TPU v7x, 256 devices: a whole 4x4x8 slice. The times are simulated.
256 devices in a mesh: dom: 64 (over z, x, core), sub: 4 (over y).
Axes of the slice: x: 4, y: 4, z: 8, core: 2. Of those that a mesh axis runs over, the one named last changes fastest.
Arguments:
- flow_pops: float32 [512, 19, 512], P(('dom', 'sub')), may hold values from 0 to 0.5, as said below
- bin_pops: float32 [512, 84, 512], P(('dom', 'sub')), may hold values from 0 to 1, as said below
- site_kind: int32 [512, 512], P(('dom', 'sub')), may hold values from 0 to 3, as said below
- neighbours: int32 [512, 18], P(('dom', 'sub')), may hold values from -1 to 511, as said below
- bin_rates: float32 [12], replicated, may hold values from 0.8 to 1.9
- settle: float32 [12], replicated, may hold values from 0.005 to 0.05
- inlet_conc: float32 [12], replicated, may hold values from 0.3 to 3
Outputs:
- flow_out: float32 [512, 19, 512], P(('dom', 'sub'))
- bins_out: float32 [512, 84, 512], P(('dom', 'sub'))
- deposit: float32 [512, 12], P(('dom', 'sub'))
Inputs may be any that keep to these rules, and one draw needn't show every extreme that they name: `site_kind`: 0 solid, 1 fluid, 2 inlet (the first layer of sites along the segment), 3 outlet (the last). `neighbours`: relations are mutual; a block and its neighbour are held by devices at most 3 apart in the order of dom+sub, and that distance is reached. Blocks are numbered layer by layer along the segment, so a layer's blocks lie on two consecutive devices. `flow_pops`: positive. `bin_pops`: positive.
All inputs are finite; a program needn't handle non-finite values.
Results may differ from a plain program's by a relative error of at most 0.0003.
Values sent between devices are 32-bit elements; how exact they have to be, the bound alone decides.
A program may use at most 64 MiB of HBM per device.

v0:
```python
import functools

import jax
import jax.numpy as jnp
from jax import lax
from jax.experimental import pallas as pl
from jax.experimental.pallas import tpu as pltpu
from jax.sharding import PartitionSpec as P

VEL = [
    (0, 0, 0),
    (1, 0, 0),
    (-1, 0, 0),
    (0, 1, 0),
    (0, -1, 0),
    (0, 0, 1),
    (0, 0, -1),
    (1, 1, 0),
    (-1, -1, 0),
    (1, -1, 0),
    (-1, 1, 0),
    (1, 0, 1),
    (-1, 0, -1),
    (1, 0, -1),
    (-1, 0, 1),
    (0, 1, 1),
    (0, -1, -1),
    (0, 1, -1),
    (0, -1, 1),
]
WEIGHT = [1.0 / 3.0] + [1.0 / 18.0] * 6 + [1.0 / 36.0] * 12
OPP = [0, 2, 1, 4, 3, 6, 5, 8, 7, 10, 9, 12, 11, 14, 13, 16, 15, 18, 17]
OMEGA = 1.6
INLET = 0.04
BINS = 12
STEPS = 2
MESH = pl.DeviceIdType.MESH

FACE_POPS = [
    [q for q in range(1, 19) if VEL[q][d // 2] == 1 - 2 * (d % 2)] for d in range(6)
]
LIVE_SLOT = 5
BIN_SLOT = 6
PACKS = 3
LAT_ROWS, Z_ROWS = 4 * PACKS * 8, PACKS * 8


def lat_row(h):
    return 8 + LAT_ROWS * h


def z_row(way, h):
    return 8 + Z_ROWS * (2 * way + h)


def roll_lanes(x, shift):
    shift %= 128
    return x if shift == 0 else pltpu.roll(x, shift, 1)


def roll_rows(x, shift):
    shift %= 8
    return x if shift == 0 else pltpu.roll(x, shift, 0)


def kernel(
    layers,
    subs,
    flow_in,
    bins_in,
    kind_ref,
    near_ref,
    rates_ref,
    settle_ref,
    conc_ref,
    flow_out,
    bins_out,
    dep_ref,
    fbuf,
    gbuf,
    pf,
    pg,
    live_ref,
    dmask_ref,
    dacc,
    lat_0,
    lat_1,
    zwin_0,
    zwin_1,
    zsend,
    in_sem,
    out_sem,
    send_sem,
    recv_sem,
):
    lats, zwins = (lat_0, lat_1), (zwin_0, zwin_1)
    me = lax.axis_index("dom") * subs + lax.axis_index("sub")
    layer = me // 2
    half = me % 2
    has_up = layer < layers - 1
    has_down = layer > 0

    def device(g):
        return (g // subs, g % subs)

    mate = 2 * layer + 1 - half

    loads = [
        pltpu.make_async_copy(flow_in, fbuf, in_sem.at[0]),
        pltpu.make_async_copy(bins_in, gbuf, in_sem.at[1]),
    ]
    for copy in loads:
        copy.start()

    barrier = pltpu.get_barrier_semaphore()
    pl.semaphore_signal(barrier, inc=1, device_id=device(mate), device_id_type=MESH)

    @pl.when(has_up)
    def _():
        for h in range(2):
            pl.semaphore_signal(
                barrier, inc=1, device_id=device(2 * layer + 2 + h), device_id_type=MESH
            )

    @pl.when(has_down)
    def _():
        for h in range(2):
            pl.semaphore_signal(
                barrier, inc=1, device_id=device(2 * layer - 2 + h), device_id_type=MESH
            )

    sub = lax.broadcasted_iota(jnp.int32, (8, 128), 0)
    lane = lax.broadcasted_iota(jnp.int32, (8, 128), 1)
    jj = (lane >> 3) & 7
    kk = lane & 7
    low = lane < 64
    even = (sub & 1) == 0
    quarter = sub >> 1
    at = {
        (0, 0): (quarter == 0) & low,
        (0, 7): (quarter == 3) & (lane >= 64),
        (1, 0): jj == 0,
        (1, 7): jj == 7,
        (2, 0): kk == 0,
        (2, 7): kk == 7,
    }

    kind = kind_ref[...]
    alive = jnp.where(kind > 0, 1.0, 0.0)
    is_in = kind == 2
    is_out = kind == 3
    is_fluid = kind == 1

    def moments(f):
        rho = f[0]
        for q in range(1, 19):
            rho = rho + f[q]
        inv = 1.0 / rho
        vel = []
        for axis in range(3):
            plus = [f[q] for q in range(19) if VEL[q][axis] == 1]
            minus = [f[q] for q in range(19) if VEL[q][axis] == -1]
            vel.append((functools.reduce(jnp.add, plus) - functools.reduce(jnp.add, minus)) * inv)
        return rho, vel

    def equilibrium(scale, vel):
        base = 1.0 - 1.5 * (vel[0] * vel[0] + vel[1] * vel[1] + vel[2] * vel[2])
        scaled = {w: scale * w for w in set(WEIGHT)}
        out = [None] * 19
        out[0] = scaled[WEIGHT[0]] * base
        for q in range(1, 19, 2):
            along = None
            for axis in range(3):
                if VEL[q][axis] != 0:
                    term = vel[axis]
                    if along is None:
                        along = term if VEL[q][axis] > 0 else -term
                    else:
                        along = along + term if VEL[q][axis] > 0 else along - term
            even = base + 4.5 * along * along
            odd = 3.0 * along
            out[q] = scaled[WEIGHT[q]] * (even + odd)
            out[q + 1] = scaled[WEIGHT[q]] * (even - odd)
        return out

    def put(packs, d, slot, x):
        axis, minus = d // 2, d % 2
        v, m = slot // 8, slot % 8
        if axis == 0:
            t, h = m // 2, m % 2
            src_row, src_half = (0, 0) if minus else (3, 1)
            x = roll_rows(roll_lanes(x, 64 * (h - src_half)), 2 * (t - src_row))
            mask = (quarter == t) & (low if h == 0 else lane >= 64)
        else:
            src = 0 if minus else 7
            x = roll_lanes(x, (m - src) * (8 if axis == 1 else 1))
            mask = (jj if axis == 1 else kk) == m
        packs[v] = x if packs[v] is None else jnp.where(mask, x, packs[v])

    def gather(ref, row, stride, base, q):
        parts = []
        for b in range(2):
            w = jnp.clip(near_ref[b, q - 1] - base, 0, 3)
            parts.append(ref[pl.ds(row + stride * (w >> 1) + (w & 1) - b, 8), :])
        return jnp.where(even, parts[0], parts[1])

    def present(q):
        return jnp.where(even, near_ref[0, q - 1], near_ref[1, q - 1]) >= 0

    def x_shift(r, cx):
        if cx == 0:
            return r
        moved = roll_rows(r, 2 * cx)
        return jnp.where(low, moved, r) if cx > 0 else jnp.where(low, r, moved)

    def local(a, q):
        cx, cy, cz = VEL[q]
        return x_shift(roll_lanes(a, 64 * abs(cx) + 8 * cy + cz), cx)

    def unpack(d, slot, tile, q):
        cx, cy, cz = VEL[q]
        m = slot % 8
        plus = d % 2 == 0
        if d // 2 == 0:
            t, h = m // 2, m % 2
            to_row, to_half = (0, 0) if plus else (3, 1)
            return roll_rows(roll_lanes(tile, 64 * (to_half - h) + 8 * cy + cz), 2 * (to_row - t))
        to = 0 if plus else 7
        if d // 2 == 1:
            return x_shift(roll_lanes(tile, 64 * abs(cx) + 8 * (to - m) + cz), cx)
        return x_shift(roll_lanes(tile, 64 * abs(cx) + 8 * cy + to - m), cx)

    def unpack_edge(d, slot, tile, q):
        cx, cy, cz = VEL[q]
        m = slot % 8
        to = 0 if d % 2 == 0 else 7
        shift = 8 * (to - m) if d // 2 == 1 else to - m
        if cx != 0:
            return roll_rows(roll_lanes(tile, shift + 64), -6 * cx)
        return roll_lanes(tile, shift - 56 * cy)

    def face_of(axis, sign):
        return 2 * axis + (0 if sign > 0 else 1)

    def edge_face(q):
        axis = 2 if VEL[q][2] != 0 else 1
        return face_of(axis, VEL[q][axis])

    def lo(axis, sign):
        return at[(axis, 0 if sign > 0 else 7)]

    def stream(a, q, slot_of, face_tile, edge_tile):
        out = local(a, q)
        axes = [axis for axis in range(3) if VEL[q][axis] != 0]
        for axis in axes:
            d = face_of(axis, VEL[q][axis])
            slot = slot_of(d)
            out = jnp.where(
                lo(axis, VEL[q][axis]), unpack(d, slot, face_tile(d, slot // 8), q), out
            )
        if len(axes) == 2:
            d = edge_face(q)
            slot = slot_of(d)
            mask = lo(axes[0], VEL[q][axes[0]]) & lo(axes[1], VEL[q][axes[1]])
            out = jnp.where(mask, unpack_edge(d, slot, edge_tile(q), q), out)
        return out

    def copies(step):
        def mate_copy():
            span = pl.ds(lat_row(half), LAT_ROWS)
            return pltpu.make_async_remote_copy(
                src_ref=lats[step].at[span],
                dst_ref=lats[step].at[span],
                send_sem=send_sem.at[step, 0],
                recv_sem=recv_sem.at[step, 0],
                device_id=device(mate),
                device_id_type=MESH,
            )

        def mate_in():
            span = pl.ds(lat_row(1 - half), LAT_ROWS)
            return pltpu.make_async_remote_copy(
                src_ref=lats[step].at[span],
                dst_ref=lats[step].at[span],
                send_sem=send_sem.at[step, 0],
                recv_sem=recv_sem.at[step, 0],
                device_id=device(mate),
                device_id_type=MESH,
            )

        def z_copy(way, h):
            span = pl.ds(z_row(way, half), Z_ROWS)
            return pltpu.make_async_remote_copy(
                src_ref=zsend.at[step, way],
                dst_ref=zwins[step].at[span],
                send_sem=send_sem.at[step, 1 + 2 * way + h],
                recv_sem=recv_sem.at[step, 1 + 2 * way + half],
                device_id=device(2 * layer + (2 if way == 0 else -2) + h),
                device_id_type=MESH,
            )

        def z_in(way, h):
            return pltpu.make_async_remote_copy(
                src_ref=zsend.at[step, way],
                dst_ref=zwins[step].at[pl.ds(z_row(way, h), Z_ROWS)],
                send_sem=send_sem.at[step, 1 + 2 * way + h],
                recv_sem=recv_sem.at[step, 1 + 2 * way + h],
                device_id=device(2 * layer + (-2 if way == 0 else 2) + h),
                device_id_type=MESH,
            )

        return mate_copy, mate_in, z_copy, z_in

    loads[0].wait()

    for step in range(STEPS):
        first = step == 0
        mate_copy, mate_in, z_copy, z_in = copies(step)

        f = [fbuf[q] for q in range(19)]
        rho, vel = moments(f)
        target = equilibrium(OMEGA * rho, vel)
        for q in range(19):
            pf[q] = (1.0 - OMEGA) * f[q] + target[q]

        if first:
            loads[1].wait()

        x4, y4, z4 = [4.0 * u for u in vel]
        for n in range(BINS):
            rate = rates_ref[n]
            keep = 1.0 - rate
            g = [gbuf[7 * n + i] for i in range(7)]
            conc = functools.reduce(jnp.add, g)
            part = (0.125 * rate) * conc
            pg[7 * n] = keep * g[0] + (part + part)
            for axis, u4 in ((0, x4), (1, y4 - 4.0 * settle_ref[n]), (2, z4)):
                lean = part * u4
                pg[7 * n + 1 + 2 * axis] = keep * g[1 + 2 * axis] + (part + lean)
                pg[7 * n + 2 + 2 * axis] = keep * g[2 + 2 * axis] + (part - lean)

        def packed(d):
            packs = [None] * PACKS
            for s, q in enumerate(FACE_POPS[d]):
                put(packs, d, s, pf[q])
            put(packs, d, LIVE_SLOT, alive)
            for n in range(BINS):
                put(packs, d, BIN_SLOT + n, pg[7 * n + 1 + d])
            return packs

        for way in range(2):
            for v, tile in enumerate(packed(4 + way)):
                zsend[step, way, pl.ds(8 * v, 8), :] = tile

        if first:
            pl.semaphore_wait(barrier, 1 + 2 * jnp.where(has_up, 1, 0) + 2 * jnp.where(has_down, 1, 0))

        @pl.when(has_up)
        def _():
            for h in range(2):
                z_copy(0, h).start()

        @pl.when(has_down)
        def _():
            for h in range(2):
                z_copy(1, h).start()

        own = lat_row(half)
        for d in range(4):
            for v, tile in enumerate(packed(d)):
                lats[step][pl.ds(pl.multiple_of(own + 8 * (PACKS * d + v), 8), 8), :] = tile

        mate_copy().start()

        mate_in().wait_recv()

        @pl.when(has_down)
        def _():
            for h in range(2):
                z_in(0, h).wait_recv()

        @pl.when(has_up)
        def _():
            for h in range(2):
                z_in(1, h).wait_recv()

        memo = {}

        def tile_of(q, d, v):
            if (q, d, v) not in memo:
                if d >= 4:
                    base = 4 * layer + (-4 if d == 4 else 4)
                    tile = gather(zwins[step], z_row(d - 4, 0) + 8 * v, Z_ROWS, base, q)
                else:
                    row = lat_row(0) + 8 * (PACKS * d + v)
                    tile = gather(lats[step], row, LAT_ROWS, 4 * layer, q)
                if v == 0:
                    tile = jnp.where(present(q), tile, 0.0)
                memo[(q, d, v)] = tile
            return memo[(q, d, v)]

        def face_tile(d, v):
            return tile_of(OPP[1 + d], d, v)

        def edge_tile(q):
            return tile_of(OPP[q], edge_face(q), 0)

        if first:
            for q in range(1, 19):
                lq = stream(alive, q, lambda d: LIVE_SLOT, face_tile, edge_tile)
                live_ref[q - 1] = lq
                if q <= 6:
                    dmask_ref[q - 1] = jnp.where(is_fluid & (lq < 0.5), 1.0, 0.0)

        new = [pf[0]]
        for q in range(1, 19):
            moved = stream(pf[q], q, lambda d: FACE_POPS[d].index(q), face_tile, edge_tile)
            new.append(jnp.where(live_ref[q - 1] > 0.5, moved, pf[OPP[q]]))
        rho, vel = moments(new)
        base = equilibrium(jnp.ones_like(rho), vel)
        for q in range(19):
            inlet = WEIGHT[q] * (
                1.0
                + 3.0 * VEL[q][2] * INLET
                + 4.5 * (VEL[q][2] * INLET) ** 2
                - 1.5 * INLET * INLET
            )
            old = fbuf[q]
            fbuf[q] = jnp.where(
                is_fluid, new[q], jnp.where(is_out, base[q], jnp.where(is_in, inlet, old))
            )

        x4, y4, z4 = [4.0 * u for u in vel]
        for n in range(BINS):
            fall = 4.0 * settle_ref[n]
            level = conc_ref[n]
            new = [pg[7 * n]]
            absorbed = None
            for i in range(1, 7):
                moved = stream(pg[7 * n + i], i, lambda d: BIN_SLOT + n, face_tile, edge_tile)
                new.append(jnp.where(live_ref[i - 1] > 0.5, moved, 0.0))
                term = dmask_ref[i - 1] * pg[7 * n + OPP[i]]
                absorbed = term if absorbed is None else absorbed + term
            dacc[n] = absorbed if first else dacc[n] + absorbed
            conc = functools.reduce(jnp.add, new)
            part = 0.125 * conc
            outlet = [part + part]
            inlet = [0.25 * level]
            for u4, s4 in ((x4, 0.0), (y4 - fall, -fall), (z4, 4.0 * INLET)):
                lean = part * u4
                outlet += [part + lean, part - lean]
                inlet += [0.125 * level * (1.0 + s4), 0.125 * level * (1.0 - s4)]
            for i in range(7):
                old = gbuf[7 * n + i]
                gbuf[7 * n + i] = jnp.where(
                    is_fluid,
                    new[i],
                    jnp.where(is_out, outlet[i], jnp.where(is_in, inlet[i], old)),
                )

    stores = [
        pltpu.make_async_copy(fbuf, flow_out, out_sem.at[0]),
        pltpu.make_async_copy(gbuf, bins_out, out_sem.at[1]),
    ]
    for copy in stores:
        copy.start()

    table = jnp.zeros((8, 128), jnp.float32)
    for n in range(BINS):
        table = jnp.where(lane == n, jnp.sum(dacc[n], axis=1, keepdims=True), table)
    table = table + roll_rows(table, 2)
    table = table + roll_rows(table, 4)
    dep_ref[...] = table[:2, :BINS]

    for step in range(STEPS):
        mate_copy, mate_in, z_copy, z_in = copies(step)
        mate_copy().wait_send()

        @pl.when(has_up)
        def _():
            for h in range(2):
                z_copy(0, h).wait_send()

        @pl.when(has_down)
        def _():
            for h in range(2):
                z_copy(1, h).wait_send()

    for copy in stores:
        copy.wait()


def tiled(x):
    x = x.reshape(2, -1, 4, 128)
    return x.transpose(1, 2, 0, 3).reshape(-1, 8, 128)


def untiled(x):
    return x.reshape(-1, 4, 2, 128).transpose(2, 0, 1, 3).reshape(2, -1, 512)


def on_device(flow_pops, bin_pops, site_kind, neighbours, bin_rates, settle, inlet_conc):
    subs = lax.axis_size("sub")
    layers = lax.axis_size("dom") * subs // 2
    any_space = pl.BlockSpec(memory_space=pl.ANY)
    vmem = pl.BlockSpec(memory_space=pltpu.VMEM)
    smem = pl.BlockSpec(memory_space=pltpu.SMEM)
    f32 = jnp.float32
    flow, bins, deposit = pl.pallas_call(
        functools.partial(kernel, layers, subs),
        out_shape=(
            jax.ShapeDtypeStruct((19, 8, 128), f32),
            jax.ShapeDtypeStruct((7 * BINS, 8, 128), f32),
            jax.ShapeDtypeStruct((2, BINS), f32),
        ),
        in_specs=[any_space, any_space, vmem, smem, smem, smem, smem],
        out_specs=(any_space, any_space, vmem),
        scratch_shapes=[
            pltpu.VMEM((19, 8, 128), f32),
            pltpu.VMEM((7 * BINS, 8, 128), f32),
            pltpu.VMEM((19, 8, 128), f32),
            pltpu.VMEM((7 * BINS, 8, 128), f32),
            pltpu.VMEM((18, 8, 128), f32),
            pltpu.VMEM((6, 8, 128), f32),
            pltpu.VMEM((BINS, 8, 128), f32),
            pltpu.VMEM((lat_row(2) + 8, 128), f32),
            pltpu.VMEM((lat_row(2) + 8, 128), f32),
            pltpu.VMEM((z_row(2, 0) + 8, 128), f32),
            pltpu.VMEM((z_row(2, 0) + 8, 128), f32),
            pltpu.VMEM((STEPS, 2, Z_ROWS, 128), f32),
            pltpu.SemaphoreType.DMA((2,)),
            pltpu.SemaphoreType.DMA((2,)),
            pltpu.SemaphoreType.DMA((STEPS, 5)),
            pltpu.SemaphoreType.DMA((STEPS, 5)),
        ],
        compiler_params=pltpu.CompilerParams(
            collective_id=0, has_side_effects=True, vmem_limit_bytes=32 * 1024 * 1024
        ),
    )(
        tiled(flow_pops),
        tiled(bin_pops),
        tiled(site_kind)[0],
        neighbours,
        bin_rates,
        settle,
        inlet_conc,
    )
    return untiled(flow), untiled(bins), deposit


def solution(mesh):
    cut = ("dom", "sub")
    return jax.shard_map(
        on_device,
        mesh=mesh,
        in_specs=(P(cut, None, None), P(cut, None, None), P(cut, None), P(cut, None), P(), P(), P()),
        out_specs=(P(cut, None, None), P(cut, None, None), P(cut, None)),
        check_vma=False,
    )
```

profile of v0, /device:TPU:128, one launch (start us, length us, event | category | flops | bytes accessed | tf_op | source)
XLA Modules:
  0.0 23.5 jit_solution(13552396115400135535)
XLA Ops:
  0.6 0.0 copy-start.2
  0.6 0.0 copy-start.3
  0.7 0.0 copy-start.4
  0.7 0.7 %copy-done.2 = s32[2,512]{1,0:T(2,128)S(1)} copy-done((s32[2,512]{1,0:T(2,128)S(1)}, s32[2,512]{1,0:T(2,128)}, u32[]{:S(2)}) %copy-start.2) | copy-done | bytes 4120
  1.3 0.0 copy-done.3
  1.3 0.0 copy-done.4
  1.3 0.0 copy-start
  1.3 1.0 %copy-done = f32[2,84,512]{2,0,1:T(2,128)S(1)} copy-done((f32[2,84,512]{2,0,1:T(2,128)S(1)}, f32[2,84,512]{2,0,1:T(2,128)}, u32[]{:S(2)}) %copy-start) | copy-done | bytes 344088
  2.3 0.0 copy-start.1
  2.3 0.9 %copy-done.1 = f32[2,19,512]{2,0,1:T(2,128)S(1)} copy-done((f32[2,19,512]{2,0,1:T(2,128)S(1)}, f32[2,19,512]{2,0,1:T(2,128)}, u32[]{:S(2)}) %copy-start.1) | copy-done | bytes 77848
  3.2 0.0 copy-start.5
  3.2 0.7 %copy-done.5 = f32[12]{0:T(128)S(1)} copy-done((f32[12]{0:T(128)S(1)}, f32[12]{0:T(128)}, u32[]{:S(2)}) %copy-start.5) | copy-done | bytes 72
  3.9 0.0 copy-start.6
  3.9 0.7 %copy-done.6 = f32[12]{0:T(128)S(1)} copy-done((f32[12]{0:T(128)S(1)}, f32[12]{0:T(128)}, u32[]{:S(2)}) %copy-start.6) | copy-done | bytes 72
  4.5 17.1 %shard_map.94 = (f32[19,8,128]{2,1,0:T(8,128)S(1)}, f32[84,8,128]{2,1,0:T(8,128)S(1)}, f32[2,12]{1,0:T(2,128)S(1)}) custom-call(f32[19,8,128]{2,1,0:T(8,128)S(1)} %bitcast.27, f32[84,8,128]{2,1,0:T(8,128)S(1)} %bitcast.26, s32[8,128]{1,0:T(8,128)S(1)} %bitcast.29, s32[2,18]{1,0:T(2,128)S(1)} %copy-done.3, f32[12]{0:T(128)S(1)} %copy-done.4, ...), custom_call_target="tpu_custom_call" | custom-call | tf_op jit(solution)/shard_map/pallas_call | solution.py:509
  21.6 0.6 %copy.18 = f32[2,19,512]{2,0,1:T(2,128)} copy(f32[2,19,512]{2,0,1:T(2,128)S(1)} %bitcast.28) | data formatting | bytes 155648
  22.2 0.7 %copy.19 = f32[2,84,512]{2,0,1:T(2,128)} copy(f32[2,84,512]{2,0,1:T(2,128)S(1)} %bitcast.25) | data formatting | bytes 688128
  23.0 0.6 %copy.20 = f32[2,12]{1,0:T(2,128)} copy(f32[2,12]{1,0:T(2,128)S(1)} %get-tuple-element.14) | data formatting | bytes 192
Async XLA Ops:
  0.6 0.7 %copy-start.2 = (s32[2,512]{1,0:T(2,128)S(1)}, s32[2,512]{1,0:T(2,128)}, u32[]{:S(2)}) copy-start(s32[2,512]{1,0:T(2,128)} %param.9) | copy-start | bytes 12292
  0.6 0.7 %copy-start.3 = (s32[2,18]{1,0:T(2,128)S(1)}, s32[2,18]{1,0:T(2,128)}, u32[]{:S(2)}) copy-start(s32[2,18]{1,0:T(2,128)} %near_ref.1) | copy-start | bytes 436
  0.7 0.7 %copy-start.4 = (f32[12]{0:T(128)S(1)}, f32[12]{0:T(128)}, u32[]{:S(2)}) copy-start(f32[12]{0:T(128)} %rates_ref.1) | copy-start | bytes 148
  1.3 1.0 %copy-start = (f32[2,84,512]{2,0,1:T(2,128)S(1)}, f32[2,84,512]{2,0,1:T(2,128)}, u32[]{:S(2)}) copy-start(f32[2,84,512]{2,0,1:T(2,128)} %param.8) | copy-start | bytes 1032196
  2.3 0.9 %copy-start.1 = (f32[2,19,512]{2,0,1:T(2,128)S(1)}, f32[2,19,512]{2,0,1:T(2,128)}, u32[]{:S(2)}) copy-start(f32[2,19,512]{2,0,1:T(2,128)} %param.7) | copy-start | bytes 233476
  3.2 0.7 %copy-start.5 = (f32[12]{0:T(128)S(1)}, f32[12]{0:T(128)}, u32[]{:S(2)}) copy-start(f32[12]{0:T(128)} %settle_ref.1) | copy-start | bytes 148
  3.9 0.7 %copy-start.6 = (f32[12]{0:T(128)S(1)}, f32[12]{0:T(128)}, u32[]{:S(2)}) copy-start(f32[12]{0:T(128)} %conc_ref.1) | copy-start | bytes 148
where the time goes:
time: 23.7 us; the launch traced here: 23.5 us
  Pallas kernels  17.1 us (72%)
  local copies, waits for them, and re-layouts  5.77 us (24%)
  between operations  0.67 us (3%)
    pallas_call x1, Pallas kernels, on_device(): pl.pallas_call(functools.partial(kernel, layers, subs), out_shape=(jax.Sh...  17.1 us
    unnamed x17, local copies, waits for them, and re-layouts  5.77 us

commit v1 on v0

--- a/solution.py
+++ b/solution.py
@@ -68,16 +68,19 @@
     subs,
     flow_in,
     bins_in,
+    kind_in,
+    near_in,
+    rates_in,
+    settle_in,
+    conc_in,
+    fbuf,
+    gbuf,
+    dep_ref,
     kind_ref,
     near_ref,
     rates_ref,
     settle_ref,
     conc_ref,
-    flow_out,
-    bins_out,
-    dep_ref,
-    fbuf,
-    gbuf,
     pf,
     pg,
     live_ref,
@@ -89,7 +92,6 @@
     zwin_1,
     zsend,
     in_sem,
-    out_sem,
     send_sem,
     recv_sem,
 ):
@@ -105,10 +107,16 @@
 
     mate = 2 * layer + 1 - half
 
-    loads = [
-        pltpu.make_async_copy(flow_in, fbuf, in_sem.at[0]),
-        pltpu.make_async_copy(bins_in, gbuf, in_sem.at[1]),
+    pairs = [
+        (flow_in, fbuf),
+        (kind_in, kind_ref),
+        (bins_in, gbuf),
+        (rates_in, rates_ref),
+        (settle_in, settle_ref),
+        (conc_in, conc_ref),
+        (near_in, near_ref),
     ]
+    loads = [pltpu.make_async_copy(a, b, in_sem.at[n]) for n, (a, b) in enumerate(pairs)]
     for copy in loads:
         copy.start()
 
@@ -145,6 +153,8 @@
         (2, 7): kk == 7,
     }
 
+    loads[0].wait()
+    loads[1].wait()
     kind = kind_ref[...]
     alive = jnp.where(kind > 0, 1.0, 0.0)
     is_in = kind == 2
@@ -311,8 +321,6 @@
 
         return mate_copy, mate_in, z_copy, z_in
 
-    loads[0].wait()
-
     for step in range(STEPS):
         first = step == 0
         mate_copy, mate_in, z_copy, z_in = copies(step)
@@ -324,7 +332,8 @@
             pf[q] = (1.0 - OMEGA) * f[q] + target[q]
 
         if first:
-            loads[1].wait()
+            for copy in loads[2:]:
+                copy.wait()
 
         x4, y4, z4 = [4.0 * u for u in vel]
         for n in range(BINS):
@@ -458,13 +467,6 @@
                     jnp.where(is_out, outlet[i], jnp.where(is_in, inlet[i], old)),
                 )
 
-    stores = [
-        pltpu.make_async_copy(fbuf, flow_out, out_sem.at[0]),
-        pltpu.make_async_copy(gbuf, bins_out, out_sem.at[1]),
-    ]
-    for copy in stores:
-        copy.start()
-
     table = jnp.zeros((8, 128), jnp.float32)
     for n in range(BINS):
         table = jnp.where(lane == n, jnp.sum(dacc[n], axis=1, keepdims=True), table)
@@ -486,7 +488,13 @@
             for h in range(2):
                 z_copy(1, h).wait_send()
 
-    for copy in stores:
+
+def write_out(flow, bins, deposit, flow_out, bins_out, dep_out, sem):
+    pairs = [(bins, bins_out), (flow, flow_out), (deposit, dep_out)]
+    copies = [pltpu.make_async_copy(a, b, sem.at[n]) for n, (a, b) in enumerate(pairs)]
+    for copy in copies:
+        copy.start()
+    for copy in copies:
         copy.wait()
 
 
@@ -502,22 +510,25 @@
 def on_device(flow_pops, bin_pops, site_kind, neighbours, bin_rates, settle, inlet_conc):
     subs = lax.axis_size("sub")
     layers = lax.axis_size("dom") * subs // 2
-    any_space = pl.BlockSpec(memory_space=pl.ANY)
+    hbm = pl.BlockSpec(memory_space=pltpu.HBM)
     vmem = pl.BlockSpec(memory_space=pltpu.VMEM)
-    smem = pl.BlockSpec(memory_space=pltpu.SMEM)
     f32 = jnp.float32
-    flow, bins, deposit = pl.pallas_call(
+    shapes = (
+        jax.ShapeDtypeStruct((19, 8, 128), f32),
+        jax.ShapeDtypeStruct((7 * BINS, 8, 128), f32),
+        jax.ShapeDtypeStruct((2, BINS), f32),
+    )
+    done = pl.pallas_call(
         functools.partial(kernel, layers, subs),
-        out_shape=(
-            jax.ShapeDtypeStruct((19, 8, 128), f32),
-            jax.ShapeDtypeStruct((7 * BINS, 8, 128), f32),
-            jax.ShapeDtypeStruct((2, BINS), f32),
-        ),
-        in_specs=[any_space, any_space, vmem, smem, smem, smem, smem],
-        out_specs=(any_space, any_space, vmem),
+        out_shape=shapes,
+        in_specs=[hbm] * 7,
+        out_specs=(vmem, vmem, vmem),
         scratch_shapes=[
-            pltpu.VMEM((19, 8, 128), f32),
-            pltpu.VMEM((7 * BINS, 8, 128), f32),
+            pltpu.VMEM((8, 128), jnp.int32),
+            pltpu.SMEM((2, 18), jnp.int32),
+            pltpu.SMEM((BINS,), f32),
+            pltpu.SMEM((BINS,), f32),
+            pltpu.SMEM((BINS,), f32),
             pltpu.VMEM((19, 8, 128), f32),
             pltpu.VMEM((7 * BINS, 8, 128), f32),
             pltpu.VMEM((18, 8, 128), f32),
@@ -528,23 +539,35 @@
             pltpu.VMEM((z_row(2, 0) + 8, 128), f32),
             pltpu.VMEM((z_row(2, 0) + 8, 128), f32),
             pltpu.VMEM((STEPS, 2, Z_ROWS, 128), f32),
-            pltpu.SemaphoreType.DMA((2,)),
-            pltpu.SemaphoreType.DMA((2,)),
+            pltpu.SemaphoreType.DMA((7,)),
             pltpu.SemaphoreType.DMA((STEPS, 5)),
             pltpu.SemaphoreType.DMA((STEPS, 5)),
         ],
         compiler_params=pltpu.CompilerParams(
-            collective_id=0, has_side_effects=True, vmem_limit_bytes=32 * 1024 * 1024
+            collective_id=0, has_side_effects=True, vmem_limit_bytes=16 * 1024 * 1024
         ),
     )(
-        tiled(flow_pops),
-        tiled(bin_pops),
-        tiled(site_kind)[0],
-        neighbours,
-        bin_rates,
-        settle,
-        inlet_conc,
+        *[
+            pltpu.with_memory_space_constraint(x, pltpu.HBM)
+            for x in (
+                tiled(flow_pops),
+                tiled(bin_pops),
+                tiled(site_kind)[0],
+                neighbours,
+                bin_rates,
+                settle,
+                inlet_conc,
+            )
+        ]
     )
+    flow, bins, deposit = pl.pallas_call(
+        write_out,
+        out_shape=shapes,
+        in_specs=[vmem, vmem, vmem],
+        out_specs=(hbm, hbm, hbm),
+        scratch_shapes=[pltpu.SemaphoreType.DMA((3,))],
+        compiler_params=pltpu.CompilerParams(vmem_limit_bytes=16 * 1024 * 1024),
+    )(*done)
     return untiled(flow), untiled(bins), deposit
 
 

time: 23.7 us -> 17.7 us (0.75)
  local copies, waits for them, and re-layouts: 5.77 us -> 0 us
    unnamed x17 -> x0, local copies, waits for them, and re-layouts: 5.77 us -> none
    pallas_call x1 -> x2, Pallas kernels: 17.1 us -> 17 us  [the longest x1 16.2 us: on_device(): pl.pallas_call(functools.partial(kernel, layers, subs), out_shape=shapes,...]
where the time goes in v1:
time: 17.7 us; the launch traced here: 17.6 us
  Pallas kernels  17 us (96%)
  between operations  0.64 us (4%)
    pallas_call x1, Pallas kernels, on_device(): pl.pallas_call(functools.partial(kernel, layers, subs), out_shape=shapes,...  16.2 us
    pallas_call x1, Pallas kernels, on_device(): pl.pallas_call(write_out, out_shape=shapes, in_specs=[vmem, vmem, vmem],...  0.78 us

profile of v1, /device:TPU:128, one launch (start us, length us, event | category | flops | bytes accessed | tf_op | source)
XLA Modules:
  0.0 17.6 jit_solution(9206286105861226562)
XLA Ops:
  0.6 16.2 %shard_map.94 = (f32[19,8,128]{2,1,0:T(8,128)S(1)}, f32[84,8,128]{2,1,0:T(8,128)S(1)}, f32[2,12]{1,0:T(2,128)S(1)}) custom-call(f32[19,8,128]{2,1,0:T(8,128)} %bitcast.26, f32[84,8,128]{2,1,0:T(8,128)} %bitcast.25, s32[8,128]{1,0:T(8,128)} %bitcast.27, s32[2,18]{1,0:T(2,128)} %near_in.1, f32[12]{0:T(128)} %rates_in.1, f32[12]{0:T(128)} %settle_in.1, f32[12]{0:T(128)} %conc_in.1), custom_call_target="tpu_custom_call" | custom-call | tf_op jit(solution)/shard_map/pallas_call | solution.py:521
  16.8 0.8 %shard_map.95 = (f32[19,8,128]{2,1,0:T(8,128)}, f32[84,8,128]{2,1,0:T(8,128)}, f32[2,12]{1,0:T(2,128)}) custom-call(f32[19,8,128]{2,1,0:T(8,128)S(1)} %get-tuple-element.9.flow, f32[84,8,128]{2,1,0:T(8,128)S(1)} %get-tuple-element.10.bins, f32[2,12]{1,0:T(2,128)S(1)} %get-tuple-element.11.deposit), custom_call_target="tpu_custom_call" | custom-call | tf_op jit(solution)/shard_map/pallas_call | solution.py:563

commit v2 on v1

--- a/solution.py
+++ b/solution.py
@@ -33,7 +33,6 @@
 OMEGA = 1.6
 INLET = 0.04
 BINS = 12
-STEPS = 2
 MESH = pl.DeviceIdType.MESH
 
 FACE_POPS = [
@@ -42,15 +41,29 @@
 LIVE_SLOT = 5
 BIN_SLOT = 6
 PACKS = 3
-LAT_ROWS, Z_ROWS = 4 * PACKS * 8, PACKS * 8
+PART = 5
+LAT_ROWS, Z_ROWS, PART_ROWS = 2 * PACKS * 8, PACKS * 8, PART * 8
+LATERAL = [(0, 0), (1, 0), (-1, 0), (0, 1), (0, -1)]
 
 
 def lat_row(h):
     return 8 + LAT_ROWS * h
 
 
+def own_row(h, way):
+    return 8 + Z_ROWS * (2 * h + way)
+
+
 def z_row(way, h):
     return 8 + Z_ROWS * (2 * way + h)
+
+
+def part_row(way, h):
+    return 8 + PART_ROWS * (2 * way + h)
+
+
+def slot_at(d, lateral):
+    return [VEL[q][:2] for q in FACE_POPS[d]].index(lateral)
 
 
 def roll_lanes(x, shift):
@@ -83,29 +96,52 @@
     conc_ref,
     pf,
     pg,
+    sf,
+    sg,
     live_ref,
     dmask_ref,
     dacc,
     lat_0,
     lat_1,
-    zwin_0,
-    zwin_1,
-    zsend,
+    own_z,
+    zwin,
+    pwin,
+    psend,
+    ghost,
     in_sem,
     send_sem,
     recv_sem,
+    mate_send,
+    mate_recv,
 ):
-    lats, zwins = (lat_0, lat_1), (zwin_0, zwin_1)
+    lats = (lat_0, lat_1)
     me = lax.axis_index("dom") * subs + lax.axis_index("sub")
     layer = me // 2
     half = me % 2
-    has_up = layer < layers - 1
-    has_down = layer > 0
+    mate = 2 * layer + 1 - half
+    far = 1 - (me % subs) // 2
 
     def device(g):
         return (g // subs, g % subs)
 
-    mate = 2 * layer + 1 - half
+    def beyond(way):
+        return layer + 1 - 2 * way
+
+    def each_way(do):
+        for way in (far, 1 - far):
+            there = beyond(way)
+            pl.when((there >= 0) & (there < layers))(functools.partial(do, way))
+
+    barrier = pltpu.get_barrier_semaphore()
+
+    def greet(way):
+        for h in range(2):
+            pl.semaphore_signal(
+                barrier, inc=1, device_id=device(2 * beyond(way) + h), device_id_type=MESH
+            )
+
+    each_way(greet)
+    pl.semaphore_signal(barrier, inc=1, device_id=device(mate), device_id_type=MESH)
 
     pairs = [
         (flow_in, fbuf),
@@ -119,23 +155,6 @@
     loads = [pltpu.make_async_copy(a, b, in_sem.at[n]) for n, (a, b) in enumerate(pairs)]
     for copy in loads:
         copy.start()
-
-    barrier = pltpu.get_barrier_semaphore()
-    pl.semaphore_signal(barrier, inc=1, device_id=device(mate), device_id_type=MESH)
-
-    @pl.when(has_up)
-    def _():
-        for h in range(2):
-            pl.semaphore_signal(
-                barrier, inc=1, device_id=device(2 * layer + 2 + h), device_id_type=MESH
-            )
-
-    @pl.when(has_down)
-    def _():
-        for h in range(2):
-            pl.semaphore_signal(
-                barrier, inc=1, device_id=device(2 * layer - 2 + h), device_id_type=MESH
-            )
 
     sub = lax.broadcasted_iota(jnp.int32, (8, 128), 0)
     lane = lax.broadcasted_iota(jnp.int32, (8, 128), 1)
@@ -207,12 +226,14 @@
             mask = (jj if axis == 1 else kk) == m
         packs[v] = x if packs[v] is None else jnp.where(mask, x, packs[v])
 
-    def gather(ref, row, stride, base, q):
-        parts = []
-        for b in range(2):
-            w = jnp.clip(near_ref[b, q - 1] - base, 0, 3)
-            parts.append(ref[pl.ds(row + stride * (w >> 1) + (w & 1) - b, 8), :])
+    def gather(ref, row, stride, blocks):
+        parts = [
+            ref[pl.ds(row + stride * (w >> 1) + (w & 1) - b, 8), :] for b, w in enumerate(blocks)
+        ]
         return jnp.where(even, parts[0], parts[1])
+
+    def nearby(q, base):
+        return [jnp.clip(near_ref[b, q - 1] - base, 0, 3) for b in range(2)]
 
     def present(q):
         return jnp.where(even, near_ref[0, q - 1], near_ref[1, q - 1]) >= 0
@@ -275,66 +296,77 @@
             out = jnp.where(mask, unpack_edge(d, slot, edge_tile(q), q), out)
         return out
 
-    def copies(step):
-        def mate_copy():
-            span = pl.ds(lat_row(half), LAT_ROWS)
-            return pltpu.make_async_remote_copy(
-                src_ref=lats[step].at[span],
-                dst_ref=lats[step].at[span],
-                send_sem=send_sem.at[step, 0],
-                recv_sem=recv_sem.at[step, 0],
-                device_id=device(mate),
-                device_id_type=MESH,
-            )
-
-        def mate_in():
-            span = pl.ds(lat_row(1 - half), LAT_ROWS)
-            return pltpu.make_async_remote_copy(
-                src_ref=lats[step].at[span],
-                dst_ref=lats[step].at[span],
-                send_sem=send_sem.at[step, 0],
-                recv_sem=recv_sem.at[step, 0],
-                device_id=device(mate),
-                device_id_type=MESH,
-            )
-
-        def z_copy(way, h):
-            span = pl.ds(z_row(way, half), Z_ROWS)
-            return pltpu.make_async_remote_copy(
-                src_ref=zsend.at[step, way],
-                dst_ref=zwins[step].at[span],
-                send_sem=send_sem.at[step, 1 + 2 * way + h],
-                recv_sem=recv_sem.at[step, 1 + 2 * way + half],
-                device_id=device(2 * layer + (2 if way == 0 else -2) + h),
-                device_id_type=MESH,
-            )
-
-        def z_in(way, h):
-            return pltpu.make_async_remote_copy(
-                src_ref=zsend.at[step, way],
-                dst_ref=zwins[step].at[pl.ds(z_row(way, h), Z_ROWS)],
-                send_sem=send_sem.at[step, 1 + 2 * way + h],
-                recv_sem=recv_sem.at[step, 1 + 2 * way + h],
-                device_id=device(2 * layer + (-2 if way == 0 else 2) + h),
-                device_id_type=MESH,
-            )
-
-        return mate_copy, mate_in, z_copy, z_in
-
-    for step in range(STEPS):
-        first = step == 0
-        mate_copy, mate_in, z_copy, z_in = copies(step)
-
+    def mate_copy(n, ref, row, rows, h):
+        span = pl.ds(row(h), rows)
+        return pltpu.make_async_remote_copy(
+            src_ref=ref.at[span],
+            dst_ref=ref.at[span],
+            send_sem=mate_send.at[n],
+            recv_sem=mate_recv.at[n],
+            device_id=device(mate),
+            device_id_type=MESH,
+        )
+
+    def mate_copies(h):
+        return (
+            mate_copy(0, lat_0, lat_row, LAT_ROWS, h),
+            mate_copy(1, own_z, lambda h: own_row(h, 0), 2 * Z_ROWS, h),
+            mate_copy(2, lat_1, lat_row, LAT_ROWS, h),
+        )
+
+    def z_copy(n, way, h):
+        src = (own_z.at[pl.ds(own_row(half, way), Z_ROWS)], psend.at[way])[n]
+        dst = (
+            zwin.at[pl.ds(z_row(way, half), Z_ROWS)],
+            pwin.at[pl.ds(part_row(way, half), PART_ROWS)],
+        )[n]
+        return pltpu.make_async_remote_copy(
+            src_ref=src,
+            dst_ref=dst,
+            send_sem=send_sem.at[n, 2 * way + h],
+            recv_sem=recv_sem.at[n, 2 * way + half],
+            device_id=device(2 * beyond(way) + h),
+            device_id_type=MESH,
+        )
+
+    def z_in(n, way, h):
+        src = (own_z.at[pl.ds(own_row(half, way), Z_ROWS)], psend.at[way])[n]
+        dst = (
+            zwin.at[pl.ds(z_row(way, h), Z_ROWS)],
+            pwin.at[pl.ds(part_row(way, h), PART_ROWS)],
+        )[n]
+        return pltpu.make_async_remote_copy(
+            src_ref=src,
+            dst_ref=dst,
+            send_sem=send_sem.at[n, 2 * way + h],
+            recv_sem=recv_sem.at[n, 2 * way + h],
+            device_id=device(2 * beyond(1 - way) + h),
+            device_id_type=MESH,
+        )
+
+    def send_z(n):
+        def do(way):
+            for h in range(2):
+                z_copy(n, way, h).start()
+
+        each_way(do)
+
+    def receive_z(n):
+        def do(way):
+            for h in range(2):
+                z_in(n, 1 - way, h).wait_recv()
+
+        each_way(do)
+
+    def collide(first):
         f = [fbuf[q] for q in range(19)]
         rho, vel = moments(f)
         target = equilibrium(OMEGA * rho, vel)
         for q in range(19):
             pf[q] = (1.0 - OMEGA) * f[q] + target[q]
-
         if first:
             for copy in loads[2:]:
                 copy.wait()
-
         x4, y4, z4 = [4.0 * u for u in vel]
         for n in range(BINS):
             rate = rates_ref[n]
@@ -348,83 +380,72 @@
                 pg[7 * n + 1 + 2 * axis] = keep * g[1 + 2 * axis] + (part + lean)
                 pg[7 * n + 2 + 2 * axis] = keep * g[2 + 2 * axis] + (part - lean)
 
-        def packed(d):
-            packs = [None] * PACKS
-            for s, q in enumerate(FACE_POPS[d]):
-                put(packs, d, s, pf[q])
-            put(packs, d, LIVE_SLOT, alive)
-            for n in range(BINS):
-                put(packs, d, BIN_SLOT + n, pg[7 * n + 1 + d])
-            return packs
-
-        for way in range(2):
-            for v, tile in enumerate(packed(4 + way)):
-                zsend[step, way, pl.ds(8 * v, 8), :] = tile
-
-        if first:
-            pl.semaphore_wait(barrier, 1 + 2 * jnp.where(has_up, 1, 0) + 2 * jnp.where(has_down, 1, 0))
-
-        @pl.when(has_up)
-        def _():
-            for h in range(2):
-                z_copy(0, h).start()
-
-        @pl.when(has_down)
-        def _():
-            for h in range(2):
-                z_copy(1, h).start()
-
-        own = lat_row(half)
-        for d in range(4):
-            for v, tile in enumerate(packed(d)):
-                lats[step][pl.ds(pl.multiple_of(own + 8 * (PACKS * d + v), 8), 8), :] = tile
-
-        mate_copy().start()
-
-        mate_in().wait_recv()
-
-        @pl.when(has_down)
-        def _():
-            for h in range(2):
-                z_in(0, h).wait_recv()
-
-        @pl.when(has_up)
-        def _():
-            for h in range(2):
-                z_in(1, h).wait_recv()
-
+    def pack_z(way):
+        d = 4 + way
+        packs = [None] * PACKS
+        for s, q in enumerate(FACE_POPS[d]):
+            put(packs, d, s, pf[q])
+        put(packs, d, LIVE_SLOT, alive)
+        for n in range(BINS):
+            put(packs, d, BIN_SLOT + n, pg[7 * n + 1 + d])
+        for v, tile in enumerate(packs):
+            own_z[pl.ds(pl.multiple_of(own_row(half, way) + 8 * v, 8), 8), :] = tile
+
+    def pack_lateral(ref):
+        for axis in range(2):
+            sides = []
+            for d in (2 * axis, 2 * axis + 1):
+                packs = [None] * PACKS
+                for s, q in enumerate(FACE_POPS[d]):
+                    put(packs, d, s, pf[q])
+                put(packs, d, LIVE_SLOT, alive)
+                for n in range(BINS):
+                    put(packs, d, BIN_SLOT + n, pg[7 * n + 1 + d])
+                sides.append(packs)
+            ahead = present(1 + 2 * axis)
+            row = lat_row(half) + 8 * PACKS * axis
+            for v in range(PACKS):
+                ref[pl.ds(pl.multiple_of(row + 8 * v, 8), 8), :] = jnp.where(
+                    ahead, sides[0][v], sides[1][v]
+                )
+
+    def absent_as_zero(q, v, tile):
+        return jnp.where(present(q), tile, 0.0) if v == 0 else tile
+
+    def windows(lat, z_tile):
         memo = {}
 
         def tile_of(q, d, v):
             if (q, d, v) not in memo:
                 if d >= 4:
-                    base = 4 * layer + (-4 if d == 4 else 4)
-                    tile = gather(zwins[step], z_row(d - 4, 0) + 8 * v, Z_ROWS, base, q)
+                    tile = z_tile(q, d - 4, v)
                 else:
-                    row = lat_row(0) + 8 * (PACKS * d + v)
-                    tile = gather(lats[step], row, LAT_ROWS, 4 * layer, q)
-                if v == 0:
-                    tile = jnp.where(present(q), tile, 0.0)
-                memo[(q, d, v)] = tile
+                    row = lat_row(0) + 8 * (PACKS * (d // 2) + v)
+                    tile = gather(lat, row, LAT_ROWS, nearby(q, 4 * layer))
+                memo[(q, d, v)] = absent_as_zero(q, v, tile)
             return memo[(q, d, v)]
 
-        def face_tile(d, v):
-            return tile_of(OPP[1 + d], d, v)
-
-        def edge_tile(q):
-            return tile_of(OPP[q], edge_face(q), 0)
-
-        if first:
-            for q in range(1, 19):
-                lq = stream(alive, q, lambda d: LIVE_SLOT, face_tile, edge_tile)
-                live_ref[q - 1] = lq
-                if q <= 6:
-                    dmask_ref[q - 1] = jnp.where(is_fluid & (lq < 0.5), 1.0, 0.0)
-
-        new = [pf[0]]
-        for q in range(1, 19):
-            moved = stream(pf[q], q, lambda d: FACE_POPS[d].index(q), face_tile, edge_tile)
-            new.append(jnp.where(live_ref[q - 1] > 0.5, moved, pf[OPP[q]]))
+        return (
+            lambda d, v: tile_of(OPP[1 + d], d, v),
+            lambda q: tile_of(OPP[q], edge_face(q), 0),
+        )
+
+    def flow_slot(q):
+        return lambda d: FACE_POPS[d].index(q)
+
+    def bin_slot(n):
+        return lambda d: BIN_SLOT + n
+
+    def live_slot(d):
+        return LIVE_SLOT
+
+    def absorb(first):
+        for n in range(BINS):
+            terms = [dmask_ref[i - 1] * pg[7 * n + OPP[i]] for i in range(1, 7)]
+            total = functools.reduce(jnp.add, terms)
+            dacc[n] = total if first else dacc[n] + total
+
+    def settle_flow(new):
         rho, vel = moments(new)
         base = equilibrium(jnp.ones_like(rho), vel)
         for q in range(19):
@@ -438,34 +459,300 @@
             fbuf[q] = jnp.where(
                 is_fluid, new[q], jnp.where(is_out, base[q], jnp.where(is_in, inlet, old))
             )
-
-        x4, y4, z4 = [4.0 * u for u in vel]
+        return [4.0 * u for u in vel]
+
+    def settle_bins(n, new, x4, y4, z4):
+        fall = 4.0 * settle_ref[n]
+        level = conc_ref[n]
+        part = 0.125 * functools.reduce(jnp.add, new)
+        outlet = [part + part]
+        inlet = [0.25 * level]
+        for u4, s4 in ((x4, 0.0), (y4 - fall, -fall), (z4, 4.0 * INLET)):
+            lean = part * u4
+            outlet += [part + lean, part - lean]
+            inlet += [0.125 * level * (1.0 + s4), 0.125 * level * (1.0 - s4)]
+        for i in range(7):
+            old = gbuf[7 * n + i]
+            gbuf[7 * n + i] = jnp.where(
+                is_fluid, new[i], jnp.where(is_out, outlet[i], jnp.where(is_in, inlet[i], old))
+            )
+
+    collide(True)
+    for way in range(2):
+        pack_z(way)
+    ends = jnp.where(layer < layers - 1, 1, 0) + jnp.where(layer > 0, 1, 0)
+    pl.semaphore_wait(barrier, 1 + 2 * ends)
+    send_z(0)
+    pack_lateral(lat_0)
+    out_1, out_z, out_2 = mate_copies(half)
+    in_1, in_z, in_2 = mate_copies(1 - half)
+    out_1.start()
+    out_z.start()
+
+    def z_tile(q, way, v):
+        base = 4 * layer + (-4 if way == 0 else 4)
+        return gather(zwin, z_row(way, 0) + 8 * v, Z_ROWS, nearby(q, base))
+
+    in_1.wait_recv()
+    face_tile, edge_tile = windows(lat_0, z_tile)
+
+    def within(a, q, slot_of):
+        out = local(a, q)
+        axes = [axis for axis in range(2) if VEL[q][axis] != 0]
+        for axis in axes:
+            d = face_of(axis, VEL[q][axis])
+            moved = unpack(d, slot_of(d), face_tile(d, slot_of(d) // 8), q)
+            out = jnp.where(lo(axis, VEL[q][axis]), moved, out)
+        if len(axes) == 2:
+            d = edge_face(q)
+            mask = lo(0, VEL[q][0]) & lo(1, VEL[q][1])
+            out = jnp.where(mask, unpack_edge(d, slot_of(d), edge_tile(q), q), out)
+        return out
+
+    def across(a, q, slot_of):
+        cx, cy, cz = VEL[q]
+        if cz == 0:
+            return a
+        d = face_of(2, cz)
+        slot = slot_of(d)
+        moved = unpack(d, slot, face_tile(d, slot // 8), q)
+        for axis in range(2):
+            if VEL[q][axis] != 0:
+                moved = jnp.where(
+                    lo(axis, VEL[q][axis]), unpack_edge(d, slot, edge_tile(q), q), moved
+                )
+        return jnp.where(lo(2, cz), moved, a)
+
+    flow = [pf[0]]
+    for q in range(1, 19):
+        lq = within(alive, q, live_slot)
+        live_ref[q - 1] = lq
+        flow.append(jnp.where(lq > 0.5, within(pf[q], q, flow_slot(q)), pf[OPP[q]]))
+        sf[q] = flow[q]
+
+    def total(rows, pick):
+        return functools.reduce(jnp.add, [rows[q] for q in range(len(rows)) if pick(VEL[q])])
+
+    level_sum = [
+        total(flow, lambda c: c[2] == 0),
+        total(flow, lambda c: c[0] == 1 and c[2] == 0)
+        - total(flow, lambda c: c[0] == -1 and c[2] == 0),
+        total(flow, lambda c: c[1] == 1 and c[2] == 0)
+        - total(flow, lambda c: c[1] == -1 and c[2] == 0),
+    ]
+    parts = [[None] * PART for way in range(2)]
+
+    def put_part(way, tile, m, x):
+        packs = [None] * PART
+        packs[tile] = parts[way][tile]
+        put(packs, 4 + way, 8 * tile + m, x)
+        parts[way][tile] = packs[tile]
+
+    for way in range(2):
+        sign = 1 - 2 * way
+        rows = FACE_POPS[4 + way]
+        for s, q in enumerate(rows):
+            put_part(way, 0, s, flow[q])
+        put_part(way, 0, LIVE_SLOT, level_sum[0] + functools.reduce(jnp.add, [flow[q] for q in rows]))
+        x_sum = flow[rows[slot_at(4 + way, (1, 0))]] - flow[rows[slot_at(4 + way, (-1, 0))]]
+        y_sum = flow[rows[slot_at(4 + way, (0, 1))]] - flow[rows[slot_at(4 + way, (0, -1))]]
+        put_part(way, 3, 2, level_sum[1] + x_sum)
+        put_part(way, 3, 3, level_sum[2] + y_sum)
+    for n in range(BINS):
+        g = [pg[7 * n]]
+        for i in range(1, 7):
+            moved = within(pg[7 * n + i], i, bin_slot(n))
+            g.append(jnp.where(live_ref[i - 1] > 0.5, moved, 0.0))
+            sg[6 * n + i - 1] = g[i]
+        flat = functools.reduce(jnp.add, g[:5])
+        v, m = (BIN_SLOT + n) // 8, (BIN_SLOT + n) % 8
+        for way in range(2):
+            put_part(way, v, m, g[5 + way])
+            put_part(way, 4 if v == 1 else 3, m, flat + g[5 + way])
+    for way in range(2):
+        for v in range(PART):
+            psend[way, pl.ds(8 * v, 8), :] = parts[way][v]
+    send_z(1)
+
+    receive_z(0)
+    new = [pf[0]]
+    for q in range(1, 19):
+        if VEL[q][2] == 0:
+            new.append(sf[q])
+            continue
+        lq = across(live_ref[q - 1], q, live_slot)
+        live_ref[q - 1] = lq
+        border = lo(2, VEL[q][2])
+        moved = across(sf[q], q, flow_slot(q))
+        new.append(jnp.where(border & (lq < 0.5), pf[OPP[q]], moved))
+    for i in range(1, 7):
+        dmask_ref[i - 1] = jnp.where(is_fluid & (live_ref[i - 1] < 0.5), 1.0, 0.0)
+    absorb(True)
+    x4, y4, z4 = settle_flow(new)
+    for n in range(BINS):
+        new = [pg[7 * n]] + [sg[6 * n + i] for i in range(4)]
+        for i in (5, 6):
+            moved = across(sg[6 * n + i - 1], i, bin_slot(n))
+            new.append(jnp.where(live_ref[i - 1] > 0.5, moved, 0.0))
+        settle_bins(n, new, x4, y4, z4)
+    collide(False)
+    pack_lateral(lat_1)
+    out_2.start()
+
+    place = [
+        (
+            jnp.where(near_ref[b, 1] >= 0, 1, 0),
+            jnp.where(near_ref[b, 3] >= 0, 1, 0),
+        )
+        for b in range(2)
+    ]
+
+    def blocks_by_place(dz, base):
+        def pick(wanted):
+            ids = [near_ref[0, VEL.index(c) - 1] for c in wanted]
+            return jnp.clip(functools.reduce(jnp.maximum, ids) - base, 0, 3)
+
+        here = 2 * half if dz == 0 else pick([(0, 0, dz)])
+        along_x = pick([(1, 0, dz), (-1, 0, dz)])
+        along_y = pick([(0, 1, dz), (0, -1, dz)])
+        last = jnp.clip(6 - here - along_x - along_y, 0, 3)
+        px, py = place[0]
+        return [
+            [
+                jnp.where(
+                    px == x, jnp.where(py == y, here, along_y), jnp.where(py == y, along_x, last)
+                )
+                for y in range(2)
+            ]
+            for x in range(2)
+        ]
+
+    in_z.wait_recv()
+    receive_z(1)
+    mine = blocks_by_place(0, 4 * layer)
+    theirs = [blocks_by_place(-1, 4 * layer - 4), blocks_by_place(1, 4 * layer + 4)]
+    spots = [(way, y) for way in range(2) for y in range(2)]
+
+    def column(ids, y):
+        return [ids[0][y], ids[1][y]]
+
+    arriving, leaving, partial = {}, {}, {}
+    for way, y in spots:
+        for v in range(PACKS):
+            row = own_row(0, 1 - way) + 8 * v
+            arriving[way, y, v] = gather(own_z, row, 2 * Z_ROWS, column(mine, y))
+        leaving[way, y] = gather(zwin, z_row(way, 0), Z_ROWS, column(theirs[way], y))
+        for v in range(PART):
+            row = part_row(way, 0) + 8 * v
+            partial[way, y, v] = gather(pwin, row, PART_ROWS, column(theirs[way], y))
+
+    def plane(tile_at, slot_of_way):
+        out = None
+        for way, y in spots:
+            s = 2 * way + y
+            moved = roll_lanes(tile_at(way, y), s - slot_of_way(way))
+            out = moved if out is None else jnp.where(kk == s, moved, out)
+        return out
+
+    at_y = kk & 1
+
+    def plane_shift(x, lateral):
+        cx, cy = lateral
+        if cx != 0:
+            turned = roll_lanes(x, 64)
+            edge = lo(0, cx)
+            inner = edge & (~even if cx > 0 else even)
+            out = jnp.where(inner, roll_rows(turned, 3 * cx), x_shift(turned, cx))
+            return out, edge & (even if cx > 0 else ~even)
+        if cy != 0:
+            edge = lo(1, cy)
+            inner = edge & ((at_y == 1) if cy > 0 else (at_y == 0))
+            out = jnp.where(inner, roll_lanes(x, -55 * cy), roll_lanes(x, 8 * cy))
+            return out, edge & ((at_y == 0) if cy > 0 else (at_y == 1))
+        return x, None
+
+    def back(lateral):
+        return (-lateral[0], -lateral[1])
+
+    source_live = plane(lambda way, y: arriving[way, y, 0], lambda way: LIVE_SLOT)
+    came, left = {}, {}
+    for c in LATERAL:
+        left[c] = plane(lambda way, y: partial[way, y, 0], lambda way: slot_at(4 + way, c))
+        x = plane(lambda way, y: arriving[way, y, 0], lambda way: slot_at(5 - way, c))
+        bounce = plane(lambda way, y: leaving[way, y], lambda way: slot_at(4 + way, back(c)))
+        moved, outside = plane_shift(x, c)
+        lives, _ = plane_shift(source_live, c)
+        lives = lives > 0.5
+        if outside is not None:
+            lives = lives & ~outside
+        came[c] = jnp.where(lives, moved, bounce)
+    came_sum = functools.reduce(jnp.add, came.values())
+    left_sum = functools.reduce(jnp.add, left.values())
+    rho = came_sum + plane(lambda way, y: partial[way, y, 0], lambda way: LIVE_SLOT)
+    inv = 1.0 / rho
+    ux = plane(lambda way, y: partial[way, y, 3], lambda way: 2) + (came[1, 0] - came[-1, 0])
+    uy = plane(lambda way, y: partial[way, y, 3], lambda way: 3) + (came[0, 1] - came[0, -1])
+    ux, uy, un = ux * inv, uy * inv, (left_sum - came_sum) * inv
+    still = 1.0 - 1.5 * (ux * ux + uy * uy + un * un)
+    post = {}
+    for c in LATERAL:
+        along = un
+        if c[0] != 0:
+            along = along + c[0] * ux
+        if c[1] != 0:
+            along = along + c[1] * uy
+        weight = OMEGA * (WEIGHT[1] if c == (0, 0) else WEIGHT[7])
+        feq = (weight * rho) * (still + 3.0 * along + 4.5 * along * along)
+        post[c] = (1.0 - OMEGA) * left[c] + feq
+
+    def spread(x, s):
+        x = jnp.where(kk == 0, roll_lanes(x, -s), 0.0)
+        for shift in (1, 2, 4):
+            x = x + roll_lanes(x, shift)
+        return x
+
+    rate_rows = []
+    for v in range(PACKS):
+        row = jnp.zeros((8, 128), jnp.float32)
         for n in range(BINS):
-            fall = 4.0 * settle_ref[n]
-            level = conc_ref[n]
-            new = [pg[7 * n]]
-            absorbed = None
-            for i in range(1, 7):
-                moved = stream(pg[7 * n + i], i, lambda d: BIN_SLOT + n, face_tile, edge_tile)
-                new.append(jnp.where(live_ref[i - 1] > 0.5, moved, 0.0))
-                term = dmask_ref[i - 1] * pg[7 * n + OPP[i]]
-                absorbed = term if absorbed is None else absorbed + term
-            dacc[n] = absorbed if first else dacc[n] + absorbed
-            conc = functools.reduce(jnp.add, new)
-            part = 0.125 * conc
-            outlet = [part + part]
-            inlet = [0.25 * level]
-            for u4, s4 in ((x4, 0.0), (y4 - fall, -fall), (z4, 4.0 * INLET)):
-                lean = part * u4
-                outlet += [part + lean, part - lean]
-                inlet += [0.125 * level * (1.0 + s4), 0.125 * level * (1.0 - s4)]
-            for i in range(7):
-                old = gbuf[7 * n + i]
-                gbuf[7 * n + i] = jnp.where(
-                    is_fluid,
-                    new[i],
-                    jnp.where(is_out, outlet[i], jnp.where(is_in, inlet[i], old)),
-                )
+            if (BIN_SLOT + n) // 8 == v:
+                row = jnp.where(kk == (BIN_SLOT + n) % 8, rates_ref[n], row)
+        rate_rows.append(row)
+    for way, y in spots:
+        s = 2 * way + y
+        lean = 1.0 + 4.0 * spread(un, s)
+        lives = spread(source_live, s) > 0.5
+        for v in range(PACKS):
+            conc = partial[way, y, 4 if v == 1 else 3] + jnp.where(lives, arriving[way, y, v], 0.0)
+            rate = rate_rows[v]
+            tile = (1.0 - rate) * partial[way, y, v] + (0.125 * rate) * conc * lean
+            if v == 0:
+                for c in LATERAL:
+                    m = slot_at(4 + way, c)
+                    tile = jnp.where(kk == m, roll_lanes(post[c], m - s), tile)
+            ghost[pl.ds(z_row(way, y) + 8 * v, 8), :] = tile
+
+    def ghost_tile(q, way, v):
+        cx, cy, cz = VEL[q]
+        blocks = []
+        for px, py in place:
+            blocks.append(2 * (1 - py if cy != 0 else py) + (1 - px if cx != 0 else px))
+        return gather(ghost, z_row(way, 0) + 8 * v, Z_ROWS, blocks)
+
+    in_2.wait_recv()
+    face_tile, edge_tile = windows(lat_1, ghost_tile)
+    absorb(False)
+    new = [pf[0]]
+    for q in range(1, 19):
+        moved = stream(pf[q], q, flow_slot(q), face_tile, edge_tile)
+        new.append(jnp.where(live_ref[q - 1] > 0.5, moved, pf[OPP[q]]))
+    x4, y4, z4 = settle_flow(new)
+    for n in range(BINS):
+        new = [pg[7 * n]]
+        for i in range(1, 7):
+            moved = stream(pg[7 * n + i], i, bin_slot(n), face_tile, edge_tile)
+            new.append(jnp.where(live_ref[i - 1] > 0.5, moved, 0.0))
+        settle_bins(n, new, x4, y4, z4)
 
     table = jnp.zeros((8, 128), jnp.float32)
     for n in range(BINS):
@@ -474,19 +761,15 @@
     table = table + roll_rows(table, 4)
     dep_ref[...] = table[:2, :BINS]
 
-    for step in range(STEPS):
-        mate_copy, mate_in, z_copy, z_in = copies(step)
-        mate_copy().wait_send()
-
-        @pl.when(has_up)
-        def _():
+    for copy in (out_1, out_z, out_2):
+        copy.wait_send()
+
+    def sent(way):
+        for n in range(2):
             for h in range(2):
-                z_copy(0, h).wait_send()
-
-        @pl.when(has_down)
-        def _():
-            for h in range(2):
-                z_copy(1, h).wait_send()
+                z_copy(n, way, h).wait_send()
+
+    each_way(sent)
 
 
 def write_out(flow, bins, deposit, flow_out, bins_out, dep_out, sem):
@@ -531,17 +814,23 @@
             pltpu.SMEM((BINS,), f32),
             pltpu.VMEM((19, 8, 128), f32),
             pltpu.VMEM((7 * BINS, 8, 128), f32),
+            pltpu.VMEM((19, 8, 128), f32),
+            pltpu.VMEM((6 * BINS, 8, 128), f32),
             pltpu.VMEM((18, 8, 128), f32),
             pltpu.VMEM((6, 8, 128), f32),
             pltpu.VMEM((BINS, 8, 128), f32),
             pltpu.VMEM((lat_row(2) + 8, 128), f32),
             pltpu.VMEM((lat_row(2) + 8, 128), f32),
+            pltpu.VMEM((own_row(2, 0) + 8, 128), f32),
             pltpu.VMEM((z_row(2, 0) + 8, 128), f32),
+            pltpu.VMEM((part_row(2, 0) + 8, 128), f32),
+            pltpu.VMEM((2, PART_ROWS, 128), f32),
             pltpu.VMEM((z_row(2, 0) + 8, 128), f32),
-            pltpu.VMEM((STEPS, 2, Z_ROWS, 128), f32),
             pltpu.SemaphoreType.DMA((7,)),
-            pltpu.SemaphoreType.DMA((STEPS, 5)),
-            pltpu.SemaphoreType.DMA((STEPS, 5)),
+            pltpu.SemaphoreType.DMA((2, 4)),
+            pltpu.SemaphoreType.DMA((2, 4)),
+            pltpu.SemaphoreType.DMA((3,)),
+            pltpu.SemaphoreType.DMA((3,)),
         ],
         compiler_params=pltpu.CompilerParams(
             collective_id=0, has_side_effects=True, vmem_limit_bytes=16 * 1024 * 1024

time: 17.7 us -> 16.1 us (0.910)
  the two profiles are of different devices: /device:TPU:128 before, /device:TPU:127 now
where the time goes in v2:
time: 16.1 us; the launch traced here: 16 us
  Pallas kernels  15.3 us (95%)
  between operations  0.64 us (4%)
    pallas_call x1, Pallas kernels, on_device(): pl.pallas_call(functools.partial(kernel, layers, subs), out_shape=shapes,...  14.5 us
    pallas_call x1, Pallas kernels, on_device(): pl.pallas_call(write_out, out_shape=shapes, in_specs=[vmem, vmem, vmem],...  0.78 us

profile of v2, /device:TPU:127, one launch (start us, length us, event | category | flops | bytes accessed | tf_op | source)
XLA Modules:
  0.0 16.0 jit_solution(836142121645370432)
XLA Ops:
  0.6 14.5 %shard_map.94 = (f32[19,8,128]{2,1,0:T(8,128)S(1)}, f32[84,8,128]{2,1,0:T(8,128)S(1)}, f32[2,12]{1,0:T(2,128)S(1)}) custom-call(f32[19,8,128]{2,1,0:T(8,128)} %bitcast.26, f32[84,8,128]{2,1,0:T(8,128)} %bitcast.25, s32[8,128]{1,0:T(8,128)} %bitcast.27, s32[2,18]{1,0:T(2,128)} %near_in.1, f32[12]{0:T(128)} %rates_in.1, f32[12]{0:T(128)} %settle_in.1, f32[12]{0:T(128)} %conc_in.1), custom_call_target="tpu_custom_call" | custom-call | tf_op jit(solution)/shard_map/pallas_call | solution.py:804
  15.2 0.8 %shard_map.95 = (f32[19,8,128]{2,1,0:T(8,128)}, f32[84,8,128]{2,1,0:T(8,128)}, f32[2,12]{1,0:T(2,128)}) custom-call(f32[19,8,128]{2,1,0:T(8,128)S(1)} %get-tuple-element.9.flow, f32[84,8,128]{2,1,0:T(8,128)S(1)} %get-tuple-element.10.bins, f32[2,12]{1,0:T(2,128)S(1)} %get-tuple-element.11.deposit), custom_call_target="tpu_custom_call" | custom-call | tf_op jit(solution)/shard_map/pallas_call | solution.py:852

commit v3 on v2

--- a/solution.py
+++ b/solution.py
@@ -108,6 +108,7 @@
     pwin,
     psend,
     ghost,
+    came_ref,
     in_sem,
     send_sem,
     recv_sem,
@@ -281,7 +282,7 @@
         return at[(axis, 0 if sign > 0 else 7)]
 
     def stream(a, q, slot_of, face_tile, edge_tile):
-        out = local(a, q)
+        out = a
         axes = [axis for axis in range(3) if VEL[q][axis] != 0]
         for axis in axes:
             d = face_of(axis, VEL[q][axis])
@@ -477,17 +478,25 @@
                 is_fluid, new[i], jnp.where(is_out, outlet[i], jnp.where(is_in, inlet[i], old))
             )
 
+    def move_inside():
+        for q in range(1, 19):
+            sf[q] = local(pf[q], q)
+        for n in range(BINS):
+            for i in range(1, 7):
+                sg[6 * n + i - 1] = local(pg[7 * n + i], i)
+
     collide(True)
     for way in range(2):
         pack_z(way)
+    pack_lateral(lat_0)
     ends = jnp.where(layer < layers - 1, 1, 0) + jnp.where(layer > 0, 1, 0)
     pl.semaphore_wait(barrier, 1 + 2 * ends)
     send_z(0)
-    pack_lateral(lat_0)
     out_1, out_z, out_2 = mate_copies(half)
     in_1, in_z, in_2 = mate_copies(1 - half)
     out_1.start()
     out_z.start()
+    move_inside()
 
     def z_tile(q, way, v):
         base = 4 * layer + (-4 if way == 0 else 4)
@@ -497,7 +506,7 @@
     face_tile, edge_tile = windows(lat_0, z_tile)
 
     def within(a, q, slot_of):
-        out = local(a, q)
+        out = a
         axes = [axis for axis in range(2) if VEL[q][axis] != 0]
         for axis in axes:
             d = face_of(axis, VEL[q][axis])
@@ -525,9 +534,9 @@
 
     flow = [pf[0]]
     for q in range(1, 19):
-        lq = within(alive, q, live_slot)
+        lq = within(local(alive, q), q, live_slot)
         live_ref[q - 1] = lq
-        flow.append(jnp.where(lq > 0.5, within(pf[q], q, flow_slot(q)), pf[OPP[q]]))
+        flow.append(jnp.where(lq > 0.5, within(sf[q], q, flow_slot(q)), pf[OPP[q]]))
         sf[q] = flow[q]
 
     def total(rows, pick):
@@ -549,11 +558,12 @@
         parts[way][tile] = packs[tile]
 
     for way in range(2):
-        sign = 1 - 2 * way
         rows = FACE_POPS[4 + way]
         for s, q in enumerate(rows):
             put_part(way, 0, s, flow[q])
-        put_part(way, 0, LIVE_SLOT, level_sum[0] + functools.reduce(jnp.add, [flow[q] for q in rows]))
+        out_sum = functools.reduce(jnp.add, [flow[q] for q in rows])
+        put_part(way, 0, LIVE_SLOT, level_sum[0] + out_sum)
+        put_part(way, 3, 4, out_sum)
         x_sum = flow[rows[slot_at(4 + way, (1, 0))]] - flow[rows[slot_at(4 + way, (-1, 0))]]
         y_sum = flow[rows[slot_at(4 + way, (0, 1))]] - flow[rows[slot_at(4 + way, (0, -1))]]
         put_part(way, 3, 2, level_sum[1] + x_sum)
@@ -561,7 +571,7 @@
     for n in range(BINS):
         g = [pg[7 * n]]
         for i in range(1, 7):
-            moved = within(pg[7 * n + i], i, bin_slot(n))
+            moved = within(sg[6 * n + i - 1], i, bin_slot(n))
             g.append(jnp.where(live_ref[i - 1] > 0.5, moved, 0.0))
             sg[6 * n + i - 1] = g[i]
         flat = functools.reduce(jnp.add, g[:5])
@@ -598,6 +608,14 @@
     collide(False)
     pack_lateral(lat_1)
     out_2.start()
+    move_inside()
+    absorb(False)
+    table = jnp.zeros((8, 128), jnp.float32)
+    for n in range(BINS):
+        table = jnp.where(lane == n, jnp.sum(dacc[n], axis=1, keepdims=True), table)
+    table = table + roll_rows(table, 2)
+    table = table + roll_rows(table, 4)
+    dep_ref[...] = table[:2, :BINS]
 
     place = [
         (
@@ -628,7 +646,6 @@
         ]
 
     in_z.wait_recv()
-    receive_z(1)
     mine = blocks_by_place(0, 4 * layer)
     theirs = [blocks_by_place(-1, 4 * layer - 4), blocks_by_place(1, 4 * layer + 4)]
     spots = [(way, y) for way in range(2) for y in range(2)]
@@ -636,15 +653,12 @@
     def column(ids, y):
         return [ids[0][y], ids[1][y]]
 
-    arriving, leaving, partial = {}, {}, {}
+    arriving, leaving = {}, {}
     for way, y in spots:
         for v in range(PACKS):
             row = own_row(0, 1 - way) + 8 * v
             arriving[way, y, v] = gather(own_z, row, 2 * Z_ROWS, column(mine, y))
         leaving[way, y] = gather(zwin, z_row(way, 0), Z_ROWS, column(theirs[way], y))
-        for v in range(PART):
-            row = part_row(way, 0) + 8 * v
-            partial[way, y, v] = gather(pwin, row, PART_ROWS, column(theirs[way], y))
 
     def plane(tile_at, slot_of_way):
         out = None
@@ -674,10 +688,16 @@
     def back(lateral):
         return (-lateral[0], -lateral[1])
 
+    def spread(x, m):
+        out = x
+        for other in range(8):
+            if other != m:
+                out = jnp.where(kk == other, roll_lanes(x, other - m), out)
+        return out
+
     source_live = plane(lambda way, y: arriving[way, y, 0], lambda way: LIVE_SLOT)
-    came, left = {}, {}
+    came = {}
     for c in LATERAL:
-        left[c] = plane(lambda way, y: partial[way, y, 0], lambda way: slot_at(4 + way, c))
         x = plane(lambda way, y: arriving[way, y, 0], lambda way: slot_at(5 - way, c))
         bounce = plane(lambda way, y: leaving[way, y], lambda way: slot_at(4 + way, back(c)))
         moved, outside = plane_shift(x, c)
@@ -686,50 +706,61 @@
         if outside is not None:
             lives = lives & ~outside
         came[c] = jnp.where(lives, moved, bounce)
-    came_sum = functools.reduce(jnp.add, came.values())
-    left_sum = functools.reduce(jnp.add, left.values())
-    rho = came_sum + plane(lambda way, y: partial[way, y, 0], lambda way: LIVE_SLOT)
-    inv = 1.0 / rho
-    ux = plane(lambda way, y: partial[way, y, 3], lambda way: 2) + (came[1, 0] - came[-1, 0])
-    uy = plane(lambda way, y: partial[way, y, 3], lambda way: 3) + (came[0, 1] - came[0, -1])
-    ux, uy, un = ux * inv, uy * inv, (left_sum - came_sum) * inv
-    still = 1.0 - 1.5 * (ux * ux + uy * uy + un * un)
-    post = {}
-    for c in LATERAL:
-        along = un
-        if c[0] != 0:
-            along = along + c[0] * ux
-        if c[1] != 0:
-            along = along + c[1] * uy
-        weight = OMEGA * (WEIGHT[1] if c == (0, 0) else WEIGHT[7])
-        feq = (weight * rho) * (still + 3.0 * along + 4.5 * along * along)
-        post[c] = (1.0 - OMEGA) * left[c] + feq
-
-    def spread(x, s):
-        x = jnp.where(kk == 0, roll_lanes(x, -s), 0.0)
-        for shift in (1, 2, 4):
-            x = x + roll_lanes(x, shift)
-        return x
+    sums = (
+        functools.reduce(jnp.add, came.values()),
+        came[1, 0] - came[-1, 0],
+        came[0, 1] - came[0, -1],
+    )
+    for n, (way, y) in enumerate(spots):
+        s = 2 * way + y
+        for t in range(3):
+            came_ref[3 * n + t] = spread(sums[t], s)
+        lives = spread(source_live, s) > 0.5
+        for v in range(PACKS):
+            came_ref[12 + PACKS * n + v] = jnp.where(lives, arriving[way, y, v], 0.0)
+
+    def by_slot(value_of):
+        row = jnp.zeros((8, 128), jnp.float32)
+        for m in range(8):
+            if value_of(m) is not None:
+                row = jnp.where(kk == m, value_of(m), row)
+        return row
 
     rate_rows = []
     for v in range(PACKS):
-        row = jnp.zeros((8, 128), jnp.float32)
-        for n in range(BINS):
-            if (BIN_SLOT + n) // 8 == v:
-                row = jnp.where(kk == (BIN_SLOT + n) % 8, rates_ref[n], row)
-        rate_rows.append(row)
-    for way, y in spots:
-        s = 2 * way + y
-        lean = 1.0 + 4.0 * spread(un, s)
-        lives = spread(source_live, s) > 0.5
+        bins = [8 * v + m - BIN_SLOT for m in range(8)]
+        rate_rows.append(by_slot(lambda m: rates_ref[bins[m]] if 0 <= bins[m] < BINS else None))
+    weights = by_slot(lambda m: OMEGA * (WEIGHT[1] if m == 0 else WEIGHT[7]) if m < 5 else None)
+    leans = [
+        [
+            by_slot(lambda m: float(VEL[FACE_POPS[4 + way][m]][axis]) if m < 5 else None)
+            for axis in range(2)
+        ]
+        for way in range(2)
+    ]
+
+    receive_z(1)
+    for n, (way, y) in enumerate(spots):
+        partial = [
+            gather(pwin, part_row(way, 0) + 8 * v, PART_ROWS, column(theirs[way], y))
+            for v in range(PART)
+        ]
+        came_sum, came_x, came_y = [came_ref[3 * n + t] for t in range(3)]
+        rho = spread(partial[0], LIVE_SLOT) + came_sum
+        inv = 1.0 / rho
+        ux = (spread(partial[3], 2) + came_x) * inv
+        uy = (spread(partial[3], 3) + came_y) * inv
+        un = (spread(partial[3], 4) - came_sum) * inv
+        along = un + leans[way][0] * ux + leans[way][1] * uy
+        still = 1.0 - 1.5 * (ux * ux + uy * uy + un * un)
+        feq = (weights * rho) * (still + 3.0 * along + 4.5 * along * along)
+        lean = 1.0 + 4.0 * un
         for v in range(PACKS):
-            conc = partial[way, y, 4 if v == 1 else 3] + jnp.where(lives, arriving[way, y, v], 0.0)
+            conc = partial[4 if v == 1 else 3] + came_ref[12 + PACKS * n + v]
             rate = rate_rows[v]
-            tile = (1.0 - rate) * partial[way, y, v] + (0.125 * rate) * conc * lean
+            tile = (1.0 - rate) * partial[v] + (0.125 * rate) * conc * lean
             if v == 0:
-                for c in LATERAL:
-                    m = slot_at(4 + way, c)
-                    tile = jnp.where(kk == m, roll_lanes(post[c], m - s), tile)
+                tile = jnp.where(kk < 5, (1.0 - OMEGA) * partial[0] + feq, tile)
             ghost[pl.ds(z_row(way, y) + 8 * v, 8), :] = tile
 
     def ghost_tile(q, way, v):
@@ -741,25 +772,17 @@
 
     in_2.wait_recv()
     face_tile, edge_tile = windows(lat_1, ghost_tile)
-    absorb(False)
     new = [pf[0]]
     for q in range(1, 19):
-        moved = stream(pf[q], q, flow_slot(q), face_tile, edge_tile)
+        moved = stream(sf[q], q, flow_slot(q), face_tile, edge_tile)
         new.append(jnp.where(live_ref[q - 1] > 0.5, moved, pf[OPP[q]]))
     x4, y4, z4 = settle_flow(new)
     for n in range(BINS):
         new = [pg[7 * n]]
         for i in range(1, 7):
-            moved = stream(pg[7 * n + i], i, bin_slot(n), face_tile, edge_tile)
+            moved = stream(sg[6 * n + i - 1], i, bin_slot(n), face_tile, edge_tile)
             new.append(jnp.where(live_ref[i - 1] > 0.5, moved, 0.0))
         settle_bins(n, new, x4, y4, z4)
-
-    table = jnp.zeros((8, 128), jnp.float32)
-    for n in range(BINS):
-        table = jnp.where(lane == n, jnp.sum(dacc[n], axis=1, keepdims=True), table)
-    table = table + roll_rows(table, 2)
-    table = table + roll_rows(table, 4)
-    dep_ref[...] = table[:2, :BINS]
 
     for copy in (out_1, out_z, out_2):
         copy.wait_send()
@@ -826,6 +849,7 @@
             pltpu.VMEM((part_row(2, 0) + 8, 128), f32),
             pltpu.VMEM((2, PART_ROWS, 128), f32),
             pltpu.VMEM((z_row(2, 0) + 8, 128), f32),
+            pltpu.VMEM((12 + 4 * PACKS, 8, 128), f32),
             pltpu.SemaphoreType.DMA((7,)),
             pltpu.SemaphoreType.DMA((2, 4)),
             pltpu.SemaphoreType.DMA((2, 4)),

time: 16.1 us -> 15.2 us (0.944)
  the two profiles are of different devices: /device:TPU:127 before, /device:TPU:128 now
where the time goes in v3:
time: 15.2 us; the launch traced here: 15 us
  Pallas kernels  14.4 us (95%)
  between operations  0.64 us (4%)
    pallas_call x1, Pallas kernels, on_device(): pl.pallas_call(functools.partial(kernel, layers, subs), out_shape=shapes,...  13.6 us
    pallas_call x1, Pallas kernels, on_device(): pl.pallas_call(write_out, out_shape=shapes, in_specs=[vmem, vmem, vmem],...  0.78 us

profile of v3, /device:TPU:128, one launch (start us, length us, event | category | flops | bytes accessed | tf_op | source)
XLA Modules:
  0.0 15.0 jit_solution(3409503350684829777)
XLA Ops:
  0.6 13.6 %shard_map.94 = (f32[19,8,128]{2,1,0:T(8,128)S(1)}, f32[84,8,128]{2,1,0:T(8,128)S(1)}, f32[2,12]{1,0:T(2,128)S(1)}) custom-call(f32[19,8,128]{2,1,0:T(8,128)} %bitcast.26, f32[84,8,128]{2,1,0:T(8,128)} %bitcast.25, s32[8,128]{1,0:T(8,128)} %bitcast.27, s32[2,18]{1,0:T(2,128)} %near_in.1, f32[12]{0:T(128)} %rates_in.1, f32[12]{0:T(128)} %settle_in.1, f32[12]{0:T(128)} %conc_in.1), custom_call_target="tpu_custom_call" | custom-call | tf_op jit(solution)/shard_map/pallas_call | solution.py:827
  14.3 0.8 %shard_map.95 = (f32[19,8,128]{2,1,0:T(8,128)}, f32[84,8,128]{2,1,0:T(8,128)}, f32[2,12]{1,0:T(2,128)}) custom-call(f32[19,8,128]{2,1,0:T(8,128)S(1)} %get-tuple-element.9.flow, f32[84,8,128]{2,1,0:T(8,128)S(1)} %get-tuple-element.10.bins, f32[2,12]{1,0:T(2,128)S(1)} %get-tuple-element.11.deposit), custom_call_target="tpu_custom_call" | custom-call | tf_op jit(solution)/shard_map/pallas_call | solution.py:876

commit v4 on v3

--- a/solution.py
+++ b/solution.py
@@ -64,6 +64,14 @@
 
 def slot_at(d, lateral):
     return [VEL[q][:2] for q in FACE_POPS[d]].index(lateral)
+
+
+def add_up(terms):
+    terms = list(terms)
+    while len(terms) > 1:
+        pairs = [a + b for a, b in zip(terms[::2], terms[1::2])]
+        terms = pairs + terms[len(pairs) * 2 :]
+    return terms[0]
 
 
 def roll_lanes(x, shift):
@@ -178,19 +186,19 @@
     kind = kind_ref[...]
     alive = jnp.where(kind > 0, 1.0, 0.0)
     is_in = kind == 2
-    is_out = kind == 3
+    is_end = kind >= 2
     is_fluid = kind == 1
 
     def moments(f):
-        rho = f[0]
-        for q in range(1, 19):
-            rho = rho + f[q]
+        odd = range(1, 19, 2)
+        rho = add_up([f[q] + f[q + 1] for q in odd] + [f[0]])
         inv = 1.0 / rho
+        gaps = {q: f[q] - f[q + 1] for q in odd}
         vel = []
         for axis in range(3):
-            plus = [f[q] for q in range(19) if VEL[q][axis] == 1]
-            minus = [f[q] for q in range(19) if VEL[q][axis] == -1]
-            vel.append((functools.reduce(jnp.add, plus) - functools.reduce(jnp.add, minus)) * inv)
+            plus = add_up([gaps[q] for q in odd if VEL[q][axis] == 1])
+            minus = [gaps[q] for q in odd if VEL[q][axis] == -1]
+            vel.append((plus - add_up(minus) if minus else plus) * inv)
         return rho, vel
 
     def equilibrium(scale, vel):
@@ -347,7 +355,7 @@
 
     def send_z(n):
         def do(way):
-            for h in range(2):
+            for h in (half, 1 - half):
                 z_copy(n, way, h).start()
 
         each_way(do)
@@ -359,27 +367,44 @@
 
         each_way(do)
 
-    def collide(first):
+    def collide_bin(n, g, conc, rate, lean4):
+        part = (0.125 * rate) * conc
+        keep = 1.0 - rate
+        pg[7 * n] = keep * g[0] + (part + part)
+        x4, y4, z4 = lean4
+        for axis, u4 in ((0, x4), (1, y4 - 4.0 * settle_ref[n]), (2, z4)):
+            lean = part * u4
+            pg[7 * n + 1 + 2 * axis] = keep * g[1 + 2 * axis] + (part + lean)
+            pg[7 * n + 2 + 2 * axis] = keep * g[2 + 2 * axis] + (part - lean)
+
+    def collide_inputs():
         f = [fbuf[q] for q in range(19)]
         rho, vel = moments(f)
         target = equilibrium(OMEGA * rho, vel)
         for q in range(19):
             pf[q] = (1.0 - OMEGA) * f[q] + target[q]
-        if first:
-            for copy in loads[2:]:
-                copy.wait()
-        x4, y4, z4 = [4.0 * u for u in vel]
+        for copy in loads[2:]:
+            copy.wait()
+        lean4 = [4.0 * u for u in vel]
         for n in range(BINS):
-            rate = rates_ref[n]
-            keep = 1.0 - rate
             g = [gbuf[7 * n + i] for i in range(7)]
-            conc = functools.reduce(jnp.add, g)
-            part = (0.125 * rate) * conc
-            pg[7 * n] = keep * g[0] + (part + part)
-            for axis, u4 in ((0, x4), (1, y4 - 4.0 * settle_ref[n]), (2, z4)):
-                lean = part * u4
-                pg[7 * n + 1 + 2 * axis] = keep * g[1 + 2 * axis] + (part + lean)
-                pg[7 * n + 2 + 2 * axis] = keep * g[2 + 2 * axis] + (part - lean)
+            collide_bin(n, g, add_up(g), rates_ref[n], lean4)
+
+    def at_ends(vel):
+        return [jnp.where(is_in, (0.0, 0.0, INLET)[axis], vel[axis]) for axis in range(3)]
+
+    def collide_moved(flow, bins_of):
+        rho, vel = moments(flow)
+        vel = at_ends(vel)
+        target = equilibrium(jnp.where(is_fluid, OMEGA * rho, 1.0), vel)
+        keep = jnp.where(is_fluid, 1.0 - OMEGA, 0.0)
+        for q in range(19):
+            pf[q] = keep * flow[q] + target[q]
+        lean4 = [4.0 * u for u in vel]
+        for n in range(BINS):
+            g = bins_of(n)
+            conc = jnp.where(is_in, conc_ref[n], add_up(g))
+            collide_bin(n, g, conc, jnp.where(is_fluid, rates_ref[n], 1.0), lean4)
 
     def pack_z(way):
         d = 4 + way
@@ -441,42 +466,27 @@
         return LIVE_SLOT
 
     def absorb(first):
+        masks = [dmask_ref[i] > 0.5 for i in range(6)]
         for n in range(BINS):
-            terms = [dmask_ref[i - 1] * pg[7 * n + OPP[i]] for i in range(1, 7)]
-            total = functools.reduce(jnp.add, terms)
+            total = add_up([jnp.where(masks[i - 1], pg[7 * n + OPP[i]], 0.0) for i in range(1, 7)])
             dacc[n] = total if first else dacc[n] + total
 
-    def settle_flow(new):
-        rho, vel = moments(new)
-        base = equilibrium(jnp.ones_like(rho), vel)
+    def finish(flow, bins_of):
+        vel = at_ends(moments(flow)[1])
+        target = equilibrium(jnp.ones_like(vel[0]), vel)
         for q in range(19):
-            inlet = WEIGHT[q] * (
-                1.0
-                + 3.0 * VEL[q][2] * INLET
-                + 4.5 * (VEL[q][2] * INLET) ** 2
-                - 1.5 * INLET * INLET
-            )
-            old = fbuf[q]
-            fbuf[q] = jnp.where(
-                is_fluid, new[q], jnp.where(is_out, base[q], jnp.where(is_in, inlet, old))
-            )
-        return [4.0 * u for u in vel]
-
-    def settle_bins(n, new, x4, y4, z4):
-        fall = 4.0 * settle_ref[n]
-        level = conc_ref[n]
-        part = 0.125 * functools.reduce(jnp.add, new)
-        outlet = [part + part]
-        inlet = [0.25 * level]
-        for u4, s4 in ((x4, 0.0), (y4 - fall, -fall), (z4, 4.0 * INLET)):
-            lean = part * u4
-            outlet += [part + lean, part - lean]
-            inlet += [0.125 * level * (1.0 + s4), 0.125 * level * (1.0 - s4)]
-        for i in range(7):
-            old = gbuf[7 * n + i]
-            gbuf[7 * n + i] = jnp.where(
-                is_fluid, new[i], jnp.where(is_out, outlet[i], jnp.where(is_in, inlet[i], old))
-            )
+            fbuf[q] = jnp.where(is_fluid, flow[q], jnp.where(is_end, target[q], fbuf[q]))
+        x4, y4, z4 = [4.0 * u for u in vel]
+        for n in range(BINS):
+            g = bins_of(n)
+            part = 0.125 * jnp.where(is_in, conc_ref[n], add_up(g))
+            target = [part + part]
+            for u4 in (x4, y4 - 4.0 * settle_ref[n], z4):
+                lean = part * u4
+                target += [part + lean, part - lean]
+            for i in range(7):
+                old = gbuf[7 * n + i]
+                gbuf[7 * n + i] = jnp.where(is_fluid, g[i], jnp.where(is_end, target[i], old))
 
     def move_inside():
         for q in range(1, 19):
@@ -485,17 +495,16 @@
             for i in range(1, 7):
                 sg[6 * n + i - 1] = local(pg[7 * n + i], i)
 
-    collide(True)
+    collide_inputs()
     for way in range(2):
         pack_z(way)
     pack_lateral(lat_0)
     ends = jnp.where(layer < layers - 1, 1, 0) + jnp.where(layer > 0, 1, 0)
     pl.semaphore_wait(barrier, 1 + 2 * ends)
-    send_z(0)
     out_1, out_z, out_2 = mate_copies(half)
     in_1, in_z, in_2 = mate_copies(1 - half)
     out_1.start()
-    out_z.start()
+    send_z(0)
     move_inside()
 
     def z_tile(q, way, v):
@@ -540,7 +549,7 @@
         sf[q] = flow[q]
 
     def total(rows, pick):
-        return functools.reduce(jnp.add, [rows[q] for q in range(len(rows)) if pick(VEL[q])])
+        return add_up([rows[q] for q in range(len(rows)) if pick(VEL[q])])
 
     level_sum = [
         total(flow, lambda c: c[2] == 0),
@@ -561,7 +570,7 @@
         rows = FACE_POPS[4 + way]
         for s, q in enumerate(rows):
             put_part(way, 0, s, flow[q])
-        out_sum = functools.reduce(jnp.add, [flow[q] for q in rows])
+        out_sum = add_up([flow[q] for q in rows])
         put_part(way, 0, LIVE_SLOT, level_sum[0] + out_sum)
         put_part(way, 3, 4, out_sum)
         x_sum = flow[rows[slot_at(4 + way, (1, 0))]] - flow[rows[slot_at(4 + way, (-1, 0))]]
@@ -574,7 +583,7 @@
             moved = within(sg[6 * n + i - 1], i, bin_slot(n))
             g.append(jnp.where(live_ref[i - 1] > 0.5, moved, 0.0))
             sg[6 * n + i - 1] = g[i]
-        flat = functools.reduce(jnp.add, g[:5])
+        flat = add_up(g[:5])
         v, m = (BIN_SLOT + n) // 8, (BIN_SLOT + n) % 8
         for way in range(2):
             put_part(way, v, m, g[5 + way])
@@ -583,6 +592,7 @@
         for v in range(PART):
             psend[way, pl.ds(8 * v, 8), :] = parts[way][v]
     send_z(1)
+    out_z.start()
 
     receive_z(0)
     new = [pf[0]]
@@ -598,14 +608,15 @@
     for i in range(1, 7):
         dmask_ref[i - 1] = jnp.where(is_fluid & (live_ref[i - 1] < 0.5), 1.0, 0.0)
     absorb(True)
-    x4, y4, z4 = settle_flow(new)
-    for n in range(BINS):
+
+    def bins_across(n):
         new = [pg[7 * n]] + [sg[6 * n + i] for i in range(4)]
         for i in (5, 6):
             moved = across(sg[6 * n + i - 1], i, bin_slot(n))
             new.append(jnp.where(live_ref[i - 1] > 0.5, moved, 0.0))
-        settle_bins(n, new, x4, y4, z4)
-    collide(False)
+        return new
+
+    collide_moved(new, bins_across)
     pack_lateral(lat_1)
     out_2.start()
     move_inside()
@@ -707,7 +718,7 @@
             lives = lives & ~outside
         came[c] = jnp.where(lives, moved, bounce)
     sums = (
-        functools.reduce(jnp.add, came.values()),
+        add_up(came.values()),
         came[1, 0] - came[-1, 0],
         came[0, 1] - came[0, -1],
     )
@@ -776,13 +787,15 @@
     for q in range(1, 19):
         moved = stream(sf[q], q, flow_slot(q), face_tile, edge_tile)
         new.append(jnp.where(live_ref[q - 1] > 0.5, moved, pf[OPP[q]]))
-    x4, y4, z4 = settle_flow(new)
-    for n in range(BINS):
+
+    def bins_moved(n):
         new = [pg[7 * n]]
         for i in range(1, 7):
             moved = stream(sg[6 * n + i - 1], i, bin_slot(n), face_tile, edge_tile)
             new.append(jnp.where(live_ref[i - 1] > 0.5, moved, 0.0))
-        settle_bins(n, new, x4, y4, z4)
+        return new
+
+    finish(new, bins_moved)
 
     for copy in (out_1, out_z, out_2):
         copy.wait_send()

time: 15.2 us -> 14.9 us (0.980)
  Pallas kernels: 14.4 us -> 14.1 us
    pallas_call x1, Pallas kernels: 13.6 us -> 13.4 us  [on_device(): pl.pallas_call(functools.partial(kernel, layers, subs), out_shape=shapes,...]
where the time goes in v4:
time: 14.9 us; the launch traced here: 14.8 us
  Pallas kernels  14.1 us (95%)
  between operations  0.64 us (4%)
    pallas_call x1, Pallas kernels, on_device(): pl.pallas_call(functools.partial(kernel, layers, subs), out_shape=shapes,...  13.4 us
    pallas_call x1, Pallas kernels, on_device(): pl.pallas_call(write_out, out_shape=shapes, in_specs=[vmem, vmem, vmem],...  0.78 us

profile of v4, /device:TPU:128, one launch (start us, length us, event | category | flops | bytes accessed | tf_op | source)
XLA Modules:
  0.0 14.8 jit_solution(3857276664958466777)
XLA Ops:
  0.6 13.4 %shard_map.94 = (f32[19,8,128]{2,1,0:T(8,128)S(1)}, f32[84,8,128]{2,1,0:T(8,128)S(1)}, f32[2,12]{1,0:T(2,128)S(1)}) custom-call(f32[19,8,128]{2,1,0:T(8,128)} %bitcast.26, f32[84,8,128]{2,1,0:T(8,128)} %bitcast.25, s32[8,128]{1,0:T(8,128)} %bitcast.27, s32[2,18]{1,0:T(2,128)} %near_in.1, f32[12]{0:T(128)} %rates_in.1, f32[12]{0:T(128)} %settle_in.1, f32[12]{0:T(128)} %conc_in.1), custom_call_target="tpu_custom_call" | custom-call | tf_op jit(solution)/shard_map/pallas_call | solution.py:840
  14.0 0.8 %shard_map.95 = (f32[19,8,128]{2,1,0:T(8,128)}, f32[84,8,128]{2,1,0:T(8,128)}, f32[2,12]{1,0:T(2,128)}) custom-call(f32[19,8,128]{2,1,0:T(8,128)S(1)} %get-tuple-element.9.flow, f32[84,8,128]{2,1,0:T(8,128)S(1)} %get-tuple-element.10.bins, f32[2,12]{1,0:T(2,128)S(1)} %get-tuple-element.11.deposit), custom_call_target="tpu_custom_call" | custom-call | tf_op jit(solution)/shard_map/pallas_call | solution.py:889

commit v5 on v4

--- a/solution.py
+++ b/solution.py
@@ -54,12 +54,12 @@
     return 8 + Z_ROWS * (2 * h + way)
 
 
-def z_row(way, h):
-    return 8 + Z_ROWS * (2 * way + h)
-
-
-def part_row(way, h):
-    return 8 + PART_ROWS * (2 * way + h)
+def z_row(h):
+    return 8 + Z_ROWS * h
+
+
+def part_row(h):
+    return 8 + PART_ROWS * h
 
 
 def slot_at(d, lateral):
@@ -103,6 +103,7 @@
     settle_ref,
     conc_ref,
     pf,
+    pg_0,
     pg,
     sf,
     sg,
@@ -112,10 +113,13 @@
     lat_0,
     lat_1,
     own_z,
-    zwin,
-    pwin,
+    zwin_0,
+    zwin_1,
+    pwin_0,
+    pwin_1,
     psend,
-    ghost,
+    ghost_0,
+    ghost_1,
     came_ref,
     in_sem,
     send_sem,
@@ -123,7 +127,7 @@
     mate_send,
     mate_recv,
 ):
-    lats = (lat_0, lat_1)
+    zwin, pwin, ghost = (zwin_0, zwin_1), (pwin_0, pwin_1), (ghost_0, ghost_1)
     me = lax.axis_index("dom") * subs + lax.axis_index("sub")
     layer = me // 2
     half = me % 2
@@ -137,9 +141,13 @@
         return layer + 1 - 2 * way
 
     def each_way(do):
-        for way in (far, 1 - far):
-            there = beyond(way)
-            pl.when((there >= 0) & (there < layers))(functools.partial(do, way))
+        for order in ((0, 1), (1, 0)):
+
+            @pl.when(far == order[0])
+            def _():
+                for way in order:
+                    there = beyond(way)
+                    pl.when((there >= 0) & (there < layers))(functools.partial(do, way))
 
     barrier = pltpu.get_barrier_semaphore()
 
@@ -222,18 +230,9 @@
         return out
 
     def put(packs, d, slot, x):
-        axis, minus = d // 2, d % 2
         v, m = slot // 8, slot % 8
-        if axis == 0:
-            t, h = m // 2, m % 2
-            src_row, src_half = (0, 0) if minus else (3, 1)
-            x = roll_rows(roll_lanes(x, 64 * (h - src_half)), 2 * (t - src_row))
-            mask = (quarter == t) & (low if h == 0 else lane >= 64)
-        else:
-            src = 0 if minus else 7
-            x = roll_lanes(x, (m - src) * (8 if axis == 1 else 1))
-            mask = (jj if axis == 1 else kk) == m
-        packs[v] = x if packs[v] is None else jnp.where(mask, x, packs[v])
+        x = roll_lanes(x, m - (0 if d % 2 else 7))
+        packs[v] = x if packs[v] is None else jnp.where(kk == m, x, packs[v])
 
     def gather(ref, row, stride, blocks):
         parts = [
@@ -260,21 +259,21 @@
     def unpack(d, slot, tile, q):
         cx, cy, cz = VEL[q]
         m = slot % 8
-        plus = d % 2 == 0
         if d // 2 == 0:
             t, h = m // 2, m % 2
-            to_row, to_half = (0, 0) if plus else (3, 1)
-            return roll_rows(roll_lanes(tile, 64 * (to_half - h) + 8 * cy + cz), 2 * (to_row - t))
-        to = 0 if plus else 7
+            turned = roll_lanes(tile, 64 * h + 8 * cy + cz)
+            return roll_rows(turned, -2 * t if d % 2 == 0 else 4 - 2 * t)
         if d // 2 == 1:
-            return x_shift(roll_lanes(tile, 64 * abs(cx) + 8 * (to - m) + cz), cx)
-        return x_shift(roll_lanes(tile, 64 * abs(cx) + 8 * cy + to - m), cx)
+            return x_shift(roll_lanes(tile, 64 * abs(cx) - 8 * m + (112 if d % 2 else 0) + cz), cx)
+        return x_shift(roll_lanes(tile, 64 * abs(cx) + 8 * cy + (7 if d % 2 else 0) - m), cx)
 
     def unpack_edge(d, slot, tile, q):
         cx, cy, cz = VEL[q]
         m = slot % 8
-        to = 0 if d % 2 == 0 else 7
-        shift = 8 * (to - m) if d // 2 == 1 else to - m
+        if d // 2 == 1:
+            shift = (112 if d % 2 else 0) - 8 * m
+        else:
+            shift = (7 if d % 2 else 0) - m
         if cx != 0:
             return roll_rows(roll_lanes(tile, shift + 64), -6 * cx)
         return roll_lanes(tile, shift - 56 * cy)
@@ -288,22 +287,6 @@
 
     def lo(axis, sign):
         return at[(axis, 0 if sign > 0 else 7)]
-
-    def stream(a, q, slot_of, face_tile, edge_tile):
-        out = a
-        axes = [axis for axis in range(3) if VEL[q][axis] != 0]
-        for axis in axes:
-            d = face_of(axis, VEL[q][axis])
-            slot = slot_of(d)
-            out = jnp.where(
-                lo(axis, VEL[q][axis]), unpack(d, slot, face_tile(d, slot // 8), q), out
-            )
-        if len(axes) == 2:
-            d = edge_face(q)
-            slot = slot_of(d)
-            mask = lo(axes[0], VEL[q][axes[0]]) & lo(axes[1], VEL[q][axes[1]])
-            out = jnp.where(mask, unpack_edge(d, slot, edge_tile(q), q), out)
-        return out
 
     def mate_copy(n, ref, row, rows, h):
         span = pl.ds(row(h), rows)
@@ -320,14 +303,15 @@
         return (
             mate_copy(0, lat_0, lat_row, LAT_ROWS, h),
             mate_copy(1, own_z, lambda h: own_row(h, 0), 2 * Z_ROWS, h),
-            mate_copy(2, lat_1, lat_row, LAT_ROWS, h),
+            mate_copy(2, lat_1, lat_row, LAT_ROWS // 2, h),
+            mate_copy(3, lat_1, lambda h: lat_row(h) + LAT_ROWS // 2, LAT_ROWS // 2, h),
         )
 
     def z_copy(n, way, h):
         src = (own_z.at[pl.ds(own_row(half, way), Z_ROWS)], psend.at[way])[n]
         dst = (
-            zwin.at[pl.ds(z_row(way, half), Z_ROWS)],
-            pwin.at[pl.ds(part_row(way, half), PART_ROWS)],
+            zwin[way].at[pl.ds(z_row(half), Z_ROWS)],
+            pwin[way].at[pl.ds(part_row(half), PART_ROWS)],
         )[n]
         return pltpu.make_async_remote_copy(
             src_ref=src,
@@ -341,8 +325,8 @@
     def z_in(n, way, h):
         src = (own_z.at[pl.ds(own_row(half, way), Z_ROWS)], psend.at[way])[n]
         dst = (
-            zwin.at[pl.ds(z_row(way, h), Z_ROWS)],
-            pwin.at[pl.ds(part_row(way, h), PART_ROWS)],
+            zwin[way].at[pl.ds(z_row(h), Z_ROWS)],
+            pwin[way].at[pl.ds(part_row(h), PART_ROWS)],
         )[n]
         return pltpu.make_async_remote_copy(
             src_ref=src,
@@ -360,14 +344,24 @@
 
         each_way(do)
 
-    def receive_z(n):
-        def do(way):
+    def receive_z(n, side):
+        @pl.when(layer > 0 if side == 0 else layer < layers - 1)
+        def _():
             for h in range(2):
-                z_in(n, 1 - way, h).wait_recv()
-
-        each_way(do)
-
-    def collide_bin(n, g, conc, rate, lean4):
+                z_in(n, side, h).wait_recv()
+
+    def nearer_first(do):
+        for order in ((0, 1), (1, 0)):
+
+            @pl.when(far == order[0])
+            def _():
+                for side in order:
+                    do(side)
+
+    def from_side(side):
+        return [q for q in range(1, 19) if VEL[q][2] == 1 - 2 * side]
+
+    def collide_bin(pg, n, g, conc, rate, lean4):
         part = (0.125 * rate) * conc
         keep = 1.0 - rate
         pg[7 * n] = keep * g[0] + (part + part)
@@ -388,7 +382,7 @@
         lean4 = [4.0 * u for u in vel]
         for n in range(BINS):
             g = [gbuf[7 * n + i] for i in range(7)]
-            collide_bin(n, g, add_up(g), rates_ref[n], lean4)
+            collide_bin(pg_0, n, g, add_up(g), rates_ref[n], lean4)
 
     def at_ends(vel):
         return [jnp.where(is_in, (0.0, 0.0, INLET)[axis], vel[axis]) for axis in range(3)]
@@ -404,7 +398,7 @@
         for n in range(BINS):
             g = bins_of(n)
             conc = jnp.where(is_in, conc_ref[n], add_up(g))
-            collide_bin(n, g, conc, jnp.where(is_fluid, rates_ref[n], 1.0), lean4)
+            collide_bin(pg, n, g, conc, jnp.where(is_fluid, rates_ref[n], 1.0), lean4)
 
     def pack_z(way):
         d = 4 + way
@@ -413,27 +407,33 @@
             put(packs, d, s, pf[q])
         put(packs, d, LIVE_SLOT, alive)
         for n in range(BINS):
-            put(packs, d, BIN_SLOT + n, pg[7 * n + 1 + d])
+            put(packs, d, BIN_SLOT + n, pg_0[7 * n + 1 + d])
         for v, tile in enumerate(packs):
             own_z[pl.ds(pl.multiple_of(own_row(half, way) + 8 * v, 8), 8), :] = tile
 
-    def pack_lateral(ref):
-        for axis in range(2):
-            sides = []
-            for d in (2 * axis, 2 * axis + 1):
-                packs = [None] * PACKS
-                for s, q in enumerate(FACE_POPS[d]):
-                    put(packs, d, s, pf[q])
-                put(packs, d, LIVE_SLOT, alive)
-                for n in range(BINS):
-                    put(packs, d, BIN_SLOT + n, pg[7 * n + 1 + d])
-                sides.append(packs)
-            ahead = present(1 + 2 * axis)
-            row = lat_row(half) + 8 * PACKS * axis
-            for v in range(PACKS):
-                ref[pl.ds(pl.multiple_of(row + 8 * v, 8), 8), :] = jnp.where(
-                    ahead, sides[0][v], sides[1][v]
-                )
+    def pack_lateral(ref, axis, pg):
+        ahead = present(1 + 2 * axis)
+        if axis == 0:
+            spot = 2 * quarter + jnp.where(low, 0, 1)
+            spot = jnp.where(ahead, spot, 2 * ((quarter + 3) & 3) + jnp.where(low, 1, 0))
+        else:
+            spot = jnp.where(ahead, jj, (jj + 7) & 7)
+        packs = [None] * PACKS
+        rows = [(pf[q], pf[r]) for q, r in zip(FACE_POPS[2 * axis], FACE_POPS[2 * axis + 1])]
+        rows.append((alive, alive))
+        for n in range(BINS):
+            rows.append((pg[7 * n + 1 + 2 * axis], pg[7 * n + 2 + 2 * axis]))
+        for slot, (x, y) in enumerate(rows):
+            v, m = slot // 8, slot % 8
+            x = jnp.where(ahead, x, y)
+            if axis == 0:
+                x = roll_rows(roll_lanes(x, 64 * (m % 2 - 1)), 2 * (m // 2 - 3))
+            else:
+                x = roll_lanes(x, 8 * (m - 7))
+            packs[v] = x if packs[v] is None else jnp.where(spot == m, x, packs[v])
+        row = lat_row(half) + 8 * PACKS * axis
+        for v in range(PACKS):
+            ref[pl.ds(pl.multiple_of(row + 8 * v, 8), 8), :] = packs[v]
 
     def absent_as_zero(q, v, tile):
         return jnp.where(present(q), tile, 0.0) if v == 0 else tile
@@ -465,7 +465,7 @@
     def live_slot(d):
         return LIVE_SLOT
 
-    def absorb(first):
+    def absorb(first, pg):
         masks = [dmask_ref[i] > 0.5 for i in range(6)]
         for n in range(BINS):
             total = add_up([jnp.where(masks[i - 1], pg[7 * n + OPP[i]], 0.0) for i in range(1, 7)])
@@ -488,7 +488,7 @@
                 old = gbuf[7 * n + i]
                 gbuf[7 * n + i] = jnp.where(is_fluid, g[i], jnp.where(is_end, target[i], old))
 
-    def move_inside():
+    def move_inside(pg):
         for q in range(1, 19):
             sf[q] = local(pf[q], q)
         for n in range(BINS):
@@ -498,18 +498,21 @@
     collide_inputs()
     for way in range(2):
         pack_z(way)
-    pack_lateral(lat_0)
+    pack_lateral(lat_0, 0, pg_0)
+    pack_lateral(lat_0, 1, pg_0)
     ends = jnp.where(layer < layers - 1, 1, 0) + jnp.where(layer > 0, 1, 0)
     pl.semaphore_wait(barrier, 1 + 2 * ends)
-    out_1, out_z, out_2 = mate_copies(half)
-    in_1, in_z, in_2 = mate_copies(1 - half)
+    out_1, out_z, out_2, out_3 = mate_copies(half)
+    in_1, in_z, in_2, in_3 = mate_copies(1 - half)
     out_1.start()
     send_z(0)
-    move_inside()
+    move_inside(pg_0)
+    for q in range(1, 19):
+        live_ref[q - 1] = local(alive, q)
 
     def z_tile(q, way, v):
         base = 4 * layer + (-4 if way == 0 else 4)
-        return gather(zwin, z_row(way, 0) + 8 * v, Z_ROWS, nearby(q, base))
+        return gather(zwin[way], z_row(0) + 8 * v, Z_ROWS, nearby(q, base))
 
     in_1.wait_recv()
     face_tile, edge_tile = windows(lat_0, z_tile)
@@ -520,7 +523,10 @@
         for axis in axes:
             d = face_of(axis, VEL[q][axis])
             moved = unpack(d, slot_of(d), face_tile(d, slot_of(d) // 8), q)
-            out = jnp.where(lo(axis, VEL[q][axis]), moved, out)
+            mask = lo(axis, VEL[q][axis])
+            if VEL[q][2] != 0:
+                mask = mask & ~lo(2, VEL[q][2])
+            out = jnp.where(mask, moved, out)
         if len(axes) == 2:
             d = edge_face(q)
             mask = lo(0, VEL[q][0]) & lo(1, VEL[q][1])
@@ -543,7 +549,7 @@
 
     flow = [pf[0]]
     for q in range(1, 19):
-        lq = within(local(alive, q), q, live_slot)
+        lq = within(live_ref[q - 1], q, live_slot)
         live_ref[q - 1] = lq
         flow.append(jnp.where(lq > 0.5, within(sf[q], q, flow_slot(q)), pf[OPP[q]]))
         sf[q] = flow[q]
@@ -578,7 +584,7 @@
         put_part(way, 3, 2, level_sum[1] + x_sum)
         put_part(way, 3, 3, level_sum[2] + y_sum)
     for n in range(BINS):
-        g = [pg[7 * n]]
+        g = [pg_0[7 * n]]
         for i in range(1, 7):
             moved = within(sg[6 * n + i - 1], i, bin_slot(n))
             g.append(jnp.where(live_ref[i - 1] > 0.5, moved, 0.0))
@@ -594,33 +600,37 @@
     send_z(1)
     out_z.start()
 
-    receive_z(0)
-    new = [pf[0]]
-    for q in range(1, 19):
-        if VEL[q][2] == 0:
-            new.append(sf[q])
-            continue
-        lq = across(live_ref[q - 1], q, live_slot)
-        live_ref[q - 1] = lq
-        border = lo(2, VEL[q][2])
-        moved = across(sf[q], q, flow_slot(q))
-        new.append(jnp.where(border & (lq < 0.5), pf[OPP[q]], moved))
+    def cross_1(side):
+        nonlocal face_tile, edge_tile
+        receive_z(0, side)
+        face_tile, edge_tile = windows(lat_0, z_tile)
+        for q in from_side(side):
+            lq = across(live_ref[q - 1], q, live_slot)
+            live_ref[q - 1] = lq
+            border = lo(2, VEL[q][2])
+            moved = across(sf[q], q, flow_slot(q))
+            sf[q] = jnp.where(border & (lq < 0.5), pf[OPP[q]], moved)
+        lives = live_ref[4 + side] > 0.5
+        for n in range(BINS):
+            moved = across(sg[6 * n + 4 + side], 5 + side, bin_slot(n))
+            sg[6 * n + 4 + side] = jnp.where(lives, moved, 0.0)
+
+    nearer_first(cross_1)
+
+    def bins_across(n):
+        return [pg_0[7 * n]] + [sg[6 * n + i] for i in range(6)]
+
+    new = [pf[0]] + [sf[q] for q in range(1, 19)]
+    collide_moved(new, bins_across)
+    pack_lateral(lat_1, 0, pg)
+    out_2.start()
+    pack_lateral(lat_1, 1, pg)
+    out_3.start()
+    move_inside(pg)
     for i in range(1, 7):
         dmask_ref[i - 1] = jnp.where(is_fluid & (live_ref[i - 1] < 0.5), 1.0, 0.0)
-    absorb(True)
-
-    def bins_across(n):
-        new = [pg[7 * n]] + [sg[6 * n + i] for i in range(4)]
-        for i in (5, 6):
-            moved = across(sg[6 * n + i - 1], i, bin_slot(n))
-            new.append(jnp.where(live_ref[i - 1] > 0.5, moved, 0.0))
-        return new
-
-    collide_moved(new, bins_across)
-    pack_lateral(lat_1)
-    out_2.start()
-    move_inside()
-    absorb(False)
+    absorb(True, pg_0)
+    absorb(False, pg)
     table = jnp.zeros((8, 128), jnp.float32)
     for n in range(BINS):
         table = jnp.where(lane == n, jnp.sum(dacc[n], axis=1, keepdims=True), table)
@@ -669,7 +679,7 @@
         for v in range(PACKS):
             row = own_row(0, 1 - way) + 8 * v
             arriving[way, y, v] = gather(own_z, row, 2 * Z_ROWS, column(mine, y))
-        leaving[way, y] = gather(zwin, z_row(way, 0), Z_ROWS, column(theirs[way], y))
+        leaving[way, y] = gather(zwin[way], z_row(0), Z_ROWS, column(theirs[way], y))
 
     def plane(tile_at, slot_of_way):
         out = None
@@ -750,54 +760,87 @@
         for way in range(2)
     ]
 
-    receive_z(1)
-    for n, (way, y) in enumerate(spots):
-        partial = [
-            gather(pwin, part_row(way, 0) + 8 * v, PART_ROWS, column(theirs[way], y))
-            for v in range(PART)
-        ]
-        came_sum, came_x, came_y = [came_ref[3 * n + t] for t in range(3)]
-        rho = spread(partial[0], LIVE_SLOT) + came_sum
-        inv = 1.0 / rho
-        ux = (spread(partial[3], 2) + came_x) * inv
-        uy = (spread(partial[3], 3) + came_y) * inv
-        un = (spread(partial[3], 4) - came_sum) * inv
-        along = un + leans[way][0] * ux + leans[way][1] * uy
-        still = 1.0 - 1.5 * (ux * ux + uy * uy + un * un)
-        feq = (weights * rho) * (still + 3.0 * along + 4.5 * along * along)
-        lean = 1.0 + 4.0 * un
-        for v in range(PACKS):
-            conc = partial[4 if v == 1 else 3] + came_ref[12 + PACKS * n + v]
-            rate = rate_rows[v]
-            tile = (1.0 - rate) * partial[v] + (0.125 * rate) * conc * lean
-            if v == 0:
-                tile = jnp.where(kk < 5, (1.0 - OMEGA) * partial[0] + feq, tile)
-            ghost[pl.ds(z_row(way, y) + 8 * v, 8), :] = tile
+    def lateral_sites():
+        in_2.wait_recv()
+        in_3.wait_recv()
+        for q in range(1, 19):
+            if VEL[q][:2] != (0, 0):
+                sf[q] = within(sf[q], q, flow_slot(q))
+        for n in range(BINS):
+            for i in range(1, 5):
+                sg[6 * n + i - 1] = within(sg[6 * n + i - 1], i, bin_slot(n))
 
     def ghost_tile(q, way, v):
         cx, cy, cz = VEL[q]
         blocks = []
         for px, py in place:
             blocks.append(2 * (1 - py if cy != 0 else py) + (1 - px if cx != 0 else px))
-        return gather(ghost, z_row(way, 0) + 8 * v, Z_ROWS, blocks)
-
-    in_2.wait_recv()
-    face_tile, edge_tile = windows(lat_1, ghost_tile)
+        return gather(ghost[way], z_row(0) + 8 * v, Z_ROWS, blocks)
+
+    core = (me // subs) % 2
+
+    @pl.when(core == 1)
+    def _():
+        nonlocal face_tile, edge_tile
+        face_tile, edge_tile = windows(lat_1, ghost_tile)
+        lateral_sites()
+
+    def ghosts(way):
+        for y in range(2):
+            n = 2 * way + y
+            partial = [
+                gather(pwin[way], part_row(0) + 8 * v, PART_ROWS, column(theirs[way], y))
+                for v in range(PART)
+            ]
+            came_sum, came_x, came_y = [came_ref[3 * n + t] for t in range(3)]
+            rho = spread(partial[0], LIVE_SLOT) + came_sum
+            inv = 1.0 / rho
+            ux = (spread(partial[3], 2) + came_x) * inv
+            uy = (spread(partial[3], 3) + came_y) * inv
+            un = (spread(partial[3], 4) - came_sum) * inv
+            along = un + leans[way][0] * ux + leans[way][1] * uy
+            still = 1.0 - 1.5 * (ux * ux + uy * uy + un * un)
+            feq = (weights * rho) * (still + 3.0 * along + 4.5 * along * along)
+            lean = 1.0 + 4.0 * un
+            for v in range(PACKS):
+                conc = partial[4 if v == 1 else 3] + came_ref[12 + PACKS * n + v]
+                rate = rate_rows[v]
+                tile = (1.0 - rate) * partial[v] + (0.125 * rate) * conc * lean
+                if v == 0:
+                    tile = jnp.where(kk < 5, (1.0 - OMEGA) * partial[0] + feq, tile)
+                ghost[way][pl.ds(z_row(y) + 8 * v, 8), :] = tile
+
+    def cross_2(side):
+        nonlocal face_tile, edge_tile
+        receive_z(1, side)
+        ghosts(side)
+        face_tile, edge_tile = windows(lat_1, ghost_tile)
+        for q in from_side(side):
+            sf[q] = across(sf[q], q, flow_slot(q))
+        for n in range(BINS):
+            sg[6 * n + 4 + side] = across(sg[6 * n + 4 + side], 5 + side, bin_slot(n))
+
+    nearer_first(cross_2)
+
+    @pl.when(core == 0)
+    def _():
+        nonlocal face_tile, edge_tile
+        face_tile, edge_tile = windows(lat_1, ghost_tile)
+        lateral_sites()
+
     new = [pf[0]]
     for q in range(1, 19):
-        moved = stream(sf[q], q, flow_slot(q), face_tile, edge_tile)
-        new.append(jnp.where(live_ref[q - 1] > 0.5, moved, pf[OPP[q]]))
+        new.append(jnp.where(live_ref[q - 1] > 0.5, sf[q], pf[OPP[q]]))
 
     def bins_moved(n):
         new = [pg[7 * n]]
         for i in range(1, 7):
-            moved = stream(sg[6 * n + i - 1], i, bin_slot(n), face_tile, edge_tile)
-            new.append(jnp.where(live_ref[i - 1] > 0.5, moved, 0.0))
+            new.append(jnp.where(live_ref[i - 1] > 0.5, sg[6 * n + i - 1], 0.0))
         return new
 
     finish(new, bins_moved)
 
-    for copy in (out_1, out_z, out_2):
+    for copy in (out_1, out_z, out_2, out_3):
         copy.wait_send()
 
     def sent(way):
@@ -850,6 +893,7 @@
             pltpu.SMEM((BINS,), f32),
             pltpu.VMEM((19, 8, 128), f32),
             pltpu.VMEM((7 * BINS, 8, 128), f32),
+            pltpu.VMEM((7 * BINS, 8, 128), f32),
             pltpu.VMEM((19, 8, 128), f32),
             pltpu.VMEM((6 * BINS, 8, 128), f32),
             pltpu.VMEM((18, 8, 128), f32),
@@ -858,16 +902,19 @@
             pltpu.VMEM((lat_row(2) + 8, 128), f32),
             pltpu.VMEM((lat_row(2) + 8, 128), f32),
             pltpu.VMEM((own_row(2, 0) + 8, 128), f32),
-            pltpu.VMEM((z_row(2, 0) + 8, 128), f32),
-            pltpu.VMEM((part_row(2, 0) + 8, 128), f32),
+            pltpu.VMEM((z_row(2) + 8, 128), f32),
+            pltpu.VMEM((z_row(2) + 8, 128), f32),
+            pltpu.VMEM((part_row(2) + 8, 128), f32),
+            pltpu.VMEM((part_row(2) + 8, 128), f32),
             pltpu.VMEM((2, PART_ROWS, 128), f32),
-            pltpu.VMEM((z_row(2, 0) + 8, 128), f32),
+            pltpu.VMEM((z_row(2) + 8, 128), f32),
+            pltpu.VMEM((z_row(2) + 8, 128), f32),
             pltpu.VMEM((12 + 4 * PACKS, 8, 128), f32),
             pltpu.SemaphoreType.DMA((7,)),
             pltpu.SemaphoreType.DMA((2, 4)),
             pltpu.SemaphoreType.DMA((2, 4)),
-            pltpu.SemaphoreType.DMA((3,)),
-            pltpu.SemaphoreType.DMA((3,)),
+            pltpu.SemaphoreType.DMA((4,)),
+            pltpu.SemaphoreType.DMA((4,)),
         ],
         compiler_params=pltpu.CompilerParams(
             collective_id=0, has_side_effects=True, vmem_limit_bytes=16 * 1024 * 1024

time: 14.9 us -> 14.9 us (level)
  no operation moved by 1% of the time
where the time goes in v5:
time: 14.9 us; the launch traced here: 14.8 us
  Pallas kernels  14.2 us (95%)
  between operations  0.64 us (4%)
    pallas_call x1, Pallas kernels, on_device(): pl.pallas_call(functools.partial(kernel, layers, subs), out_shape=shapes,...  13.4 us
    pallas_call x1, Pallas kernels, on_device(): pl.pallas_call(write_out, out_shape=shapes, in_specs=[vmem, vmem, vmem],...  0.78 us

profile of v5, /device:TPU:128, one launch (start us, length us, event | category | flops | bytes accessed | tf_op | source)
XLA Modules:
  0.0 14.8 jit_solution(7526208359789117018)
XLA Ops:
  0.6 13.4 %shard_map.94 = (f32[19,8,128]{2,1,0:T(8,128)S(1)}, f32[84,8,128]{2,1,0:T(8,128)S(1)}, f32[2,12]{1,0:T(2,128)S(1)}) custom-call(f32[19,8,128]{2,1,0:T(8,128)} %bitcast.26, f32[84,8,128]{2,1,0:T(8,128)} %bitcast.25, s32[8,128]{1,0:T(8,128)} %bitcast.27, s32[2,18]{1,0:T(2,128)} %near_in.1, f32[12]{0:T(128)} %rates_in.1, f32[12]{0:T(128)} %settle_in.1, f32[12]{0:T(128)} %conc_in.1), custom_call_target="tpu_custom_call" | custom-call | tf_op jit(solution)/shard_map/pallas_call | solution.py:883
  14.1 0.8 %shard_map.95 = (f32[19,8,128]{2,1,0:T(8,128)}, f32[84,8,128]{2,1,0:T(8,128)}, f32[2,12]{1,0:T(2,128)}) custom-call(f32[19,8,128]{2,1,0:T(8,128)S(1)} %get-tuple-element.9.flow, f32[84,8,128]{2,1,0:T(8,128)S(1)} %get-tuple-element.10.bins, f32[2,12]{1,0:T(2,128)S(1)} %get-tuple-element.11.deposit), custom_call_target="tpu_custom_call" | custom-call | tf_op jit(solution)/shard_map/pallas_call | solution.py:936

commit v6 on v5

--- a/solution.py
+++ b/solution.py
@@ -140,12 +140,12 @@
     def beyond(way):
         return layer + 1 - 2 * way
 
-    def each_way(do):
+    def each_way(do, part=slice(None)):
         for order in ((0, 1), (1, 0)):
 
             @pl.when(far == order[0])
             def _():
-                for way in order:
+                for way in order[part]:
                     there = beyond(way)
                     pl.when((there >= 0) & (there < layers))(functools.partial(do, way))
 
@@ -337,12 +337,12 @@
             device_id_type=MESH,
         )
 
-    def send_z(n):
+    def send_z(n, part=slice(None)):
         def do(way):
             for h in (half, 1 - half):
                 z_copy(n, way, h).start()
 
-        each_way(do)
+        each_way(do, part)
 
     def receive_z(n, side):
         @pl.when(layer > 0 if side == 0 else layer < layers - 1)
@@ -504,8 +504,19 @@
     pl.semaphore_wait(barrier, 1 + 2 * ends)
     out_1, out_z, out_2, out_3 = mate_copies(half)
     in_1, in_z, in_2, in_3 = mate_copies(1 - half)
-    out_1.start()
-    send_z(0)
+    core = (me // subs) % 2
+
+    @pl.when(core == 1)
+    def _():
+        send_z(0, slice(0, 1))
+        out_1.start()
+
+    @pl.when(core == 0)
+    def _():
+        out_1.start()
+        send_z(0, slice(0, 1))
+
+    send_z(0, slice(1, 2))
     move_inside(pg_0)
     for q in range(1, 19):
         live_ref[q - 1] = local(alive, q)
@@ -776,8 +787,6 @@
         for px, py in place:
             blocks.append(2 * (1 - py if cy != 0 else py) + (1 - px if cx != 0 else px))
         return gather(ghost[way], z_row(0) + 8 * v, Z_ROWS, blocks)
-
-    core = (me // subs) % 2
 
     @pl.when(core == 1)
     def _():

time: 14.9 us -> 14.9 us (level)
  no operation moved by 1% of the time
where the time goes in v6:
time: 14.9 us; the launch traced here: 14.8 us
  Pallas kernels  14.2 us (95%)
  between operations  0.64 us (4%)
    pallas_call x1, Pallas kernels, on_device(): pl.pallas_call(functools.partial(kernel, layers, subs), out_shape=shapes,...  13.4 us
    pallas_call x1, Pallas kernels, on_device(): pl.pallas_call(write_out, out_shape=shapes, in_specs=[vmem, vmem, vmem],...  0.78 us

profile of v6, /device:TPU:128, one launch (start us, length us, event | category | flops | bytes accessed | tf_op | source)
XLA Modules:
  0.0 14.8 jit_solution(7338328259378246038)
XLA Ops:
  0.6 13.4 %shard_map.94 = (f32[19,8,128]{2,1,0:T(8,128)S(1)}, f32[84,8,128]{2,1,0:T(8,128)S(1)}, f32[2,12]{1,0:T(2,128)S(1)}) custom-call(f32[19,8,128]{2,1,0:T(8,128)} %bitcast.26, f32[84,8,128]{2,1,0:T(8,128)} %bitcast.25, s32[8,128]{1,0:T(8,128)} %bitcast.27, s32[2,18]{1,0:T(2,128)} %near_in.1, f32[12]{0:T(128)} %rates_in.1, f32[12]{0:T(128)} %settle_in.1, f32[12]{0:T(128)} %conc_in.1), custom_call_target="tpu_custom_call" | custom-call | tf_op jit(solution)/shard_map/pallas_call | solution.py:892
  14.0 0.8 %shard_map.95 = (f32[19,8,128]{2,1,0:T(8,128)}, f32[84,8,128]{2,1,0:T(8,128)}, f32[2,12]{1,0:T(2,128)}) custom-call(f32[19,8,128]{2,1,0:T(8,128)S(1)} %get-tuple-element.9.flow, f32[84,8,128]{2,1,0:T(8,128)S(1)} %get-tuple-element.10.bins, f32[2,12]{1,0:T(2,128)S(1)} %get-tuple-element.11.deposit), custom_call_target="tpu_custom_call" | custom-call | tf_op jit(solution)/shard_map/pallas_call | solution.py:945

commit v7 on v6

--- a/solution.py
+++ b/solution.py
@@ -42,7 +42,7 @@
 BIN_SLOT = 6
 PACKS = 3
 PART = 5
-LAT_ROWS, Z_ROWS, PART_ROWS = 2 * PACKS * 8, PACKS * 8, PART * 8
+LAT_ROWS, Z_ROWS, PART_ROWS = (2 * PACKS - 1) * 8, PACKS * 8, PART * 8
 LATERAL = [(0, 0), (1, 0), (-1, 0), (0, 1), (0, -1)]
 
 
@@ -303,8 +303,8 @@
         return (
             mate_copy(0, lat_0, lat_row, LAT_ROWS, h),
             mate_copy(1, own_z, lambda h: own_row(h, 0), 2 * Z_ROWS, h),
-            mate_copy(2, lat_1, lat_row, LAT_ROWS // 2, h),
-            mate_copy(3, lat_1, lambda h: lat_row(h) + LAT_ROWS // 2, LAT_ROWS // 2, h),
+            mate_copy(2, lat_1, lat_row, 16, h),
+            mate_copy(3, lat_1, lambda h: lat_row(h) + 16, LAT_ROWS - 16, h),
         )
 
     def z_copy(n, way, h):
@@ -411,7 +411,7 @@
         for v, tile in enumerate(packs):
             own_z[pl.ds(pl.multiple_of(own_row(half, way) + 8 * v, 8), 8), :] = tile
 
-    def pack_lateral(ref, axis, pg):
+    def pack_lateral(ref, axis, pg, last=None):
         ahead = present(1 + 2 * axis)
         if axis == 0:
             spot = 2 * quarter + jnp.where(low, 0, 1)
@@ -431,9 +431,14 @@
             else:
                 x = roll_lanes(x, 8 * (m - 7))
             packs[v] = x if packs[v] is None else jnp.where(spot == m, x, packs[v])
-        row = lat_row(half) + 8 * PACKS * axis
-        for v in range(PACKS):
+        row = lat_row(half) + 16 * axis
+        for v in range(2):
             ref[pl.ds(pl.multiple_of(row + 8 * v, 8), 8), :] = packs[v]
+        if axis == 0:
+            return packs[2]
+        folded = jnp.where(jj < 3, packs[2], roll_lanes(roll_rows(packs[2], 4), 24))
+        folded = jnp.where(sub < 4, folded, roll_rows(last, 4))
+        ref[pl.ds(pl.multiple_of(row + 16, 8), 8), :] = folded
 
     def absent_as_zero(q, v, tile):
         return jnp.where(present(q), tile, 0.0) if v == 0 else tile
@@ -446,8 +451,13 @@
                 if d >= 4:
                     tile = z_tile(q, d - 4, v)
                 else:
-                    row = lat_row(0) + 8 * (PACKS * (d // 2) + v)
+                    row = lat_row(0) + (16 * (d // 2) + 8 * v if v < 2 else 32)
                     tile = gather(lat, row, LAT_ROWS, nearby(q, 4 * layer))
+                    if v == 2:
+                        turned = roll_rows(tile, 4)
+                        if d // 2 == 1:
+                            turned = jnp.where(sub < 4, tile, roll_lanes(turned, -24))
+                        tile = turned
                 memo[(q, d, v)] = absent_as_zero(q, v, tile)
             return memo[(q, d, v)]
 
@@ -498,8 +508,7 @@
     collide_inputs()
     for way in range(2):
         pack_z(way)
-    pack_lateral(lat_0, 0, pg_0)
-    pack_lateral(lat_0, 1, pg_0)
+    pack_lateral(lat_0, 1, pg_0, pack_lateral(lat_0, 0, pg_0))
     ends = jnp.where(layer < layers - 1, 1, 0) + jnp.where(layer > 0, 1, 0)
     pl.semaphore_wait(barrier, 1 + 2 * ends)
     out_1, out_z, out_2, out_3 = mate_copies(half)
@@ -633,9 +642,9 @@
 
     new = [pf[0]] + [sf[q] for q in range(1, 19)]
     collide_moved(new, bins_across)
-    pack_lateral(lat_1, 0, pg)
+    last = pack_lateral(lat_1, 0, pg)
     out_2.start()
-    pack_lateral(lat_1, 1, pg)
+    pack_lateral(lat_1, 1, pg, last)
     out_3.start()
     move_inside(pg)
     for i in range(1, 7):

time: 14.9 us -> 14.9 us (level)
  no operation moved by 1% of the time
where the time goes in v7:
time: 14.9 us; the launch traced here: 14.8 us
  Pallas kernels  14.2 us (95%)
  between operations  0.64 us (4%)
    pallas_call x1, Pallas kernels, on_device(): pl.pallas_call(functools.partial(kernel, layers, subs), out_shape=shapes,...  13.4 us
    pallas_call x1, Pallas kernels, on_device(): pl.pallas_call(write_out, out_shape=shapes, in_specs=[vmem, vmem, vmem],...  0.78 us

profile of v7, /device:TPU:128, one launch (start us, length us, event | category | flops | bytes accessed | tf_op | source)
XLA Modules:
  0.0 14.8 jit_solution(16841734593162094442)
XLA Ops:
  0.6 13.4 %shard_map.94 = (f32[19,8,128]{2,1,0:T(8,128)S(1)}, f32[84,8,128]{2,1,0:T(8,128)S(1)}, f32[2,12]{1,0:T(2,128)S(1)}) custom-call(f32[19,8,128]{2,1,0:T(8,128)} %bitcast.26, f32[84,8,128]{2,1,0:T(8,128)} %bitcast.25, s32[8,128]{1,0:T(8,128)} %bitcast.27, s32[2,18]{1,0:T(2,128)} %near_in.1, f32[12]{0:T(128)} %rates_in.1, f32[12]{0:T(128)} %settle_in.1, f32[12]{0:T(128)} %conc_in.1), custom_call_target="tpu_custom_call" | custom-call | tf_op jit(solution)/shard_map/pallas_call | solution.py:901
  14.0 0.8 %shard_map.95 = (f32[19,8,128]{2,1,0:T(8,128)}, f32[84,8,128]{2,1,0:T(8,128)}, f32[2,12]{1,0:T(2,128)}) custom-call(f32[19,8,128]{2,1,0:T(8,128)S(1)} %get-tuple-element.9.flow, f32[84,8,128]{2,1,0:T(8,128)S(1)} %get-tuple-element.10.bins, f32[2,12]{1,0:T(2,128)S(1)} %get-tuple-element.11.deposit), custom_call_target="tpu_custom_call" | custom-call | tf_op jit(solution)/shard_map/pallas_call | solution.py:954
